TPU v7x, 32 devices: a whole 2x2x4 slice. The times are simulated.
32 devices in a mesh: batch: 4 (over y, x), seq: 8 (over z, core).
Axes of the slice: x: 2, y: 2, z: 4, core: 2. Of those that a mesh axis runs over, the one named last changes fastest.
Arguments:
- tokens: bfloat16 [8, 2048, 1280], P('batch', 'seq'), may hold values from -6 to 6
- cotangent: bfloat16 [8, 2048, 1280], P('batch', 'seq'), may hold values from -6 to 6
- weights: float32 [6, 1280, 1280], P(None, ('batch', 'seq'))
- gains: float32 [2, 1280], P(None, ('batch', 'seq'))
- query_scale: float32 [80], replicated, may hold values from 0 to 2
- first_weights: float32 [6, 1280, 1280], P(None, ('batch', 'seq')), may hold values from -0.00048828125 to 0.00048828125
- second_weights: float32 [6, 1280, 1280], P(None, ('batch', 'seq')), may hold values from 5.0848974e-11 to 8.135836e-10
- first_gains: float32 [2, 1280], P(None, ('batch', 'seq')), may hold values from -0.0009765625 to 0.0009765625
- second_gains: float32 [2, 1280], P(None, ('batch', 'seq')), may hold values from 2.033959e-10 to 3.2543344e-09
- first_scale: float32 [80], replicated, may hold values from -0.0078125 to 0.0078125
- second_scale: float32 [80], replicated, may hold values from 1.0169795e-09 to 5.0848974e-09
- lengths: int32 [8], P('batch'), may hold values from 256 to 2048, as said below
Outputs:
- block_out: bfloat16 [8, 2048, 1280], P('batch', 'seq')
- input_grad: float32 [8, 2048, 1280], P('batch', 'seq')
- grad_norm: float32 [], replicated
- new_weights: float32 [6, 1280, 1280], P(None, ('batch', 'seq'))
- new_first_weights: float32 [6, 1280, 1280], P(None, ('batch', 'seq'))
- new_second_weights: float32 [6, 1280, 1280], P(None, ('batch', 'seq'))
- new_gains: float32 [2, 1280], P(None, ('batch', 'seq'))
- new_first_gains: float32 [2, 1280], P(None, ('batch', 'seq'))
- new_second_gains: float32 [2, 1280], P(None, ('batch', 'seq'))
- new_scale: float32 [80], replicated
- new_first_scale: float32 [80], replicated
- new_second_scale: float32 [80], replicated
- rms_stats: float32 [3], replicated
Inputs may be any that keep to these rules, and one draw needn't show every extreme that they name: `lengths`: in each run of 2 consecutive series (those of one index of batch) one series, drawn from the seed, has length 2048.
All inputs are finite; a program needn't handle non-finite values.
Results may differ from a plain program's by a relative error of at most 0.014.
The roundings to bfloat16 on the way count: a program that leaves them out, or rounds other values in their place, can miss the bound.
Values may be sent and summed in bfloat16 or wider, within the bound.
A program may use at most 512 MiB of HBM per device.

v0:
```python
import math

import jax
import jax.numpy as jnp
from jax import lax
from jax.sharding import PartitionSpec as P

STEP = 10


NORM_EPS = 1e-06
LOG_TWO_E = 1.442695
BETA_FIRST = 0.9
BETA_SECOND = 0.999
ADAM_EPS = 1e-08
MATRIX_RATE = 0.05
GAIN_RATE = 0.5
MATRIX_DECAY = 0.1
CLIP_NORM = 1.0
MASKED = -1e30


def rms_factor(values):
    return lax.rsqrt(jnp.mean(values * values, axis=-1, keepdims=True) + NORM_EPS)


def norm_back(grad_normed, normed, factor):
    return factor * (grad_normed - normed * jnp.mean(grad_normed * normed, axis=-1, keepdims=True))


def silu_slope(values):
    logistic = jax.nn.sigmoid(values)
    return logistic * (1.0 + values * (1.0 - logistic))


def split_heads(values, head_count):
    return values.reshape(values.shape[0], head_count, values.shape[1] // head_count)


def head_groups(values, group_count):
    row_count, width = values.shape
    return values.reshape(row_count, group_count, width // group_count).transpose(1, 0, 2)


def join_groups(values):
    group_count, row_count, width = values.shape
    return values.transpose(1, 0, 2).reshape(row_count, group_count * width)


def masked_scores(queries, keys_in, query_pos, key_pos, length, head_count):
    scores = jnp.einsum(
        "qhd,khd->hqk",
        split_heads(queries, head_count),
        split_heads(keys_in, head_count),
        preferred_element_type=jnp.float32,
    )
    visible = (key_pos[None, :] <= query_pos[:, None]) & (key_pos[None, :] < length)
    return jnp.where(visible[None], scores, MASKED)


def adam_update(current, gradient, moment_one, moment_two, step_rate, decay_rate):
    new_one = BETA_FIRST * moment_one + (1.0 - BETA_FIRST) * gradient
    new_two = BETA_SECOND * moment_two + (1.0 - BETA_SECOND) * gradient * gradient
    first_hat = new_one / (1.0 - BETA_FIRST**STEP)
    second_hat = new_two / (1.0 - BETA_SECOND**STEP)
    updated = current - step_rate * (
        first_hat / (jnp.sqrt(second_hat) + ADAM_EPS) + decay_rate * current
    )
    return (updated, new_one, new_two)


def body(
    tokens,
    cotangent,
    weights,
    gains,
    query_scale,
    first_weights,
    second_weights,
    first_gains,
    second_gains,
    first_scale,
    second_scale,
    lengths,
):
    series_count, shard_len, model_width = tokens.shape
    head_size = query_scale.shape[0]
    head_count = model_width // head_size
    group_count = 4
    group_heads = head_count // group_count
    query_pos = lax.axis_index("seq") * shard_len + jnp.arange(shard_len)
    low_weights = weights.astype(jnp.bfloat16)
    low_gains = gains.astype(jnp.bfloat16)
    full_weights, full_gains = (
        lax.all_gather(low_weights, ("batch", "seq"), axis=1, tiled=True),
        lax.all_gather(low_gains, ("batch", "seq"), axis=1, tiled=True),
    )
    inputs = tokens.astype(jnp.float32)
    factor_one = rms_factor(inputs)
    normed_one = inputs * factor_one
    normed_in = (normed_one * full_gains[0].astype(jnp.float32)).astype(jnp.bfloat16)
    projected = jnp.einsum(
        "std,kde->kste", normed_in, full_weights[:3], preferred_element_type=jnp.float32
    )
    coef_row = jnp.tile(LOG_TWO_E / math.sqrt(head_size) * jax.nn.softplus(query_scale), head_count)
    queries = (projected[0] * coef_row).astype(jnp.bfloat16)
    keys_own = projected[1].astype(jnp.bfloat16)
    values_own = projected[2].astype(jnp.bfloat16)
    all_keys, all_values = (
        lax.all_gather(keys_own, "seq", axis=1, tiled=True),
        lax.all_gather(values_own, "seq", axis=1, tiled=True),
    )
    full_len = all_keys.shape[1]
    key_pos = jnp.arange(full_len)

    def attend(bundle):
        rows_q, rows_k, rows_v, length = bundle

        def attend_group(inner):
            group_q, group_k, group_v = inner
            scores = masked_scores(group_q, group_k, query_pos, key_pos, length, group_heads)
            log_total = jax.nn.logsumexp(scores, axis=-1)
            attn_probs = jnp.exp(scores - log_total[:, :, None]).astype(jnp.bfloat16)
            mixed = jnp.einsum(
                "hqk,khd->qhd",
                attn_probs,
                split_heads(group_v, group_heads),
                preferred_element_type=jnp.float32,
            )
            return (mixed.reshape(shard_len, group_heads * head_size), log_total.T)

        mixed, log_rows = lax.map(
            attend_group,
            (
                head_groups(rows_q, group_count),
                head_groups(rows_k, group_count),
                head_groups(rows_v, group_count),
            ),
        )
        return (join_groups(mixed), join_groups(log_rows))

    attended, log_totals = lax.map(attend, (queries, all_keys, all_values, lengths))
    attended_low = attended.astype(jnp.bfloat16)
    branch_one = jnp.einsum(
        "std,de->ste", attended_low, full_weights[3], preferred_element_type=jnp.float32
    )
    middle = inputs + branch_one
    factor_two = rms_factor(middle)
    normed_two = middle * factor_two
    hidden_in = (normed_two * full_gains[1].astype(jnp.float32)).astype(jnp.bfloat16)
    pre_act = jnp.einsum(
        "std,de->ste", hidden_in, full_weights[4], preferred_element_type=jnp.float32
    )
    activated = jax.nn.silu(pre_act).astype(jnp.bfloat16)
    branch_two = jnp.einsum(
        "std,de->ste", activated, full_weights[5], preferred_element_type=jnp.float32
    )
    final_sum = middle + branch_two
    block_out = final_sum.astype(jnp.bfloat16)
    stat_terms = jnp.stack(
        [
            jnp.sum(branch_one * branch_one),
            jnp.sum(branch_two * branch_two),
            jnp.sum(final_sum * final_sum),
        ]
    )
    back_weights, back_gains = (
        lax.all_gather(low_weights, ("batch", "seq"), axis=1, tiled=True),
        lax.all_gather(low_gains, ("batch", "seq"), axis=1, tiled=True),
    )
    back_one = back_gains[0].astype(jnp.float32)
    back_two = back_gains[1].astype(jnp.float32)
    grad_out = cotangent.astype(jnp.float32)
    grad_down = jnp.einsum("std,ste->de", activated, cotangent, preferred_element_type=jnp.float32)
    grad_act = jnp.einsum(
        "ste,de->std", cotangent, back_weights[5], preferred_element_type=jnp.float32
    )
    grad_pre = (grad_act * silu_slope(pre_act)).astype(jnp.bfloat16)
    grad_up = jnp.einsum("std,ste->de", hidden_in, grad_pre, preferred_element_type=jnp.float32)
    grad_hidden = jnp.einsum(
        "ste,de->std", grad_pre, back_weights[4], preferred_element_type=jnp.float32
    )
    grad_gain_two = jnp.sum(grad_hidden * normed_two, axis=(0, 1))
    grad_middle = grad_out + norm_back(grad_hidden * back_two, normed_two, factor_two)
    grad_branch = grad_middle.astype(jnp.bfloat16)
    grad_out_proj = jnp.einsum(
        "std,ste->de", attended_low, grad_branch, preferred_element_type=jnp.float32
    )
    grad_attended = jnp.einsum(
        "ste,de->std", grad_branch, back_weights[3], preferred_element_type=jnp.float32
    ).astype(jnp.bfloat16)

    def query_terms(rows_q, rows_go, rows_log, rows_k, rows_v, length):
        scores = masked_scores(rows_q, rows_k, query_pos, key_pos, length, group_heads)
        attn_probs = jnp.exp(scores - rows_log.T[:, :, None])
        prob_grads = jnp.einsum(
            "qhd,khd->hqk",
            split_heads(rows_go, group_heads),
            split_heads(rows_v, group_heads),
            preferred_element_type=jnp.float32,
        )
        row_dots = jnp.sum(attn_probs * prob_grads, axis=-1)
        score_grads = (attn_probs * (prob_grads - row_dots[:, :, None])).astype(jnp.bfloat16)
        grad_rows = jnp.einsum(
            "hqk,khd->qhd",
            score_grads,
            split_heads(rows_k, group_heads),
            preferred_element_type=jnp.float32,
        )
        return (
            attn_probs,
            score_grads,
            row_dots,
            grad_rows.reshape(shard_len, group_heads * head_size),
        )

    def grouped(rows_q, rows_go, rows_log, rows_k, rows_v):
        return (
            head_groups(rows_q, group_count),
            head_groups(rows_go, group_count),
            head_groups(rows_log, group_count),
            head_groups(rows_k, group_count),
            head_groups(rows_v, group_count),
        )

    def query_full(bundle):
        rows_q, rows_go, rows_log, rows_k, rows_v, length = bundle

        def full_group(inner):
            group_q, group_go, group_log, group_k, group_v = inner
            attn_probs, score_grads, row_dots, grad_rows = query_terms(
                group_q, group_go, group_log, group_k, group_v, length
            )
            part_keys = jnp.einsum(
                "hqk,qhd->khd",
                score_grads,
                split_heads(group_q, group_heads),
                preferred_element_type=jnp.float32,
            )
            part_values = jnp.einsum(
                "hqk,qhd->khd",
                attn_probs.astype(jnp.bfloat16),
                split_heads(group_go, group_heads),
                preferred_element_type=jnp.float32,
            )
            group_width = group_heads * head_size
            return (
                grad_rows,
                part_keys.reshape(full_len, group_width),
                part_values.reshape(full_len, group_width),
            )

        grad_rows, part_keys, part_values = lax.map(
            full_group, grouped(rows_q, rows_go, rows_log, rows_k, rows_v)
        )
        return (join_groups(grad_rows), join_groups(part_keys), join_groups(part_values))

    grad_queries, keys_parts, values_parts = lax.map(
        query_full, (queries, grad_attended, log_totals, all_keys, all_values, lengths)
    )
    grad_keys, grad_values = (
        lax.psum_scatter(
            keys_parts.astype(jnp.bfloat16), "seq", scatter_dimension=1, tiled=True
        ).astype(jnp.float32),
        lax.psum_scatter(
            values_parts.astype(jnp.bfloat16), "seq", scatter_dimension=1, tiled=True
        ).astype(jnp.float32),
    )
    grad_scaled = grad_queries.astype(jnp.bfloat16).astype(jnp.float32)
    scale_slope = LOG_TWO_E / math.sqrt(head_size) * jax.nn.sigmoid(query_scale)
    scale_part = (
        jnp.sum((grad_scaled * projected[0]).reshape(-1, head_count, head_size), axis=(0, 1))
        * scale_slope
    )
    grad_query = (grad_scaled * coef_row).astype(jnp.bfloat16)
    grad_proj = jnp.stack(
        [grad_query, grad_keys.astype(jnp.bfloat16), grad_values.astype(jnp.bfloat16)]
    )
    grad_inner = jnp.einsum(
        "std,kste->kde", normed_in, grad_proj, preferred_element_type=jnp.float32
    )
    grad_normed = jnp.einsum(
        "kste,kde->std", grad_proj, back_weights[:3], preferred_element_type=jnp.float32
    )
    grad_gain_one = jnp.sum(grad_normed * normed_one, axis=(0, 1))
    input_grad = grad_middle + norm_back(grad_normed * back_one, normed_one, factor_one)
    weight_grads = jnp.concatenate(
        [grad_inner, jnp.stack([grad_out_proj, grad_up, grad_down])], axis=0
    )
    gain_grads = jnp.stack([grad_gain_one, grad_gain_two])
    own_grads, own_gain_grads = (
        lax.psum_scatter(weight_grads, ("batch", "seq"), scatter_dimension=1, tiled=True),
        lax.psum_scatter(gain_grads, ("batch", "seq"), scatter_dimension=1, tiled=True),
    )
    own_squares = jnp.sum(own_grads * own_grads) + jnp.sum(own_gain_grads * own_gain_grads)
    scale_grad = lax.psum(scale_part, ("batch", "seq"))
    leading = (lax.axis_index("batch") == 0) & (lax.axis_index("seq") == 0)
    scale_squares = jnp.where(leading, jnp.sum(scale_grad * scale_grad), 0.0)
    total_squares, stat_sums = lax.psum((own_squares + scale_squares, stat_terms), ("batch", "seq"))
    grad_norm = jnp.sqrt(total_squares)
    clip_factor = CLIP_NORM / jnp.maximum(grad_norm, CLIP_NORM)
    new_weights, new_first_weights, new_second_weights = adam_update(
        weights, own_grads * clip_factor, first_weights, second_weights, MATRIX_RATE, MATRIX_DECAY
    )
    new_gains, new_first_gains, new_second_gains = adam_update(
        gains, own_gain_grads * clip_factor, first_gains, second_gains, GAIN_RATE, 0.0
    )
    new_scale, new_first_scale, new_second_scale = adam_update(
        query_scale, scale_grad * clip_factor, first_scale, second_scale, GAIN_RATE, 0.0
    )
    position_count = float(
        series_count * shard_len * model_width * lax.axis_size("batch") * lax.axis_size("seq")
    )
    rms_stats = jnp.sqrt(stat_sums / position_count)
    return (
        block_out,
        input_grad,
        grad_norm,
        new_weights,
        new_first_weights,
        new_second_weights,
        new_gains,
        new_first_gains,
        new_second_gains,
        new_scale,
        new_first_scale,
        new_second_scale,
        rms_stats,
    )


def solution(mesh):
    return jax.shard_map(
        body,
        mesh=mesh,
        in_specs=(
            P("batch", "seq", None),
            P("batch", "seq", None),
            P(None, ("batch", "seq"), None),
            P(None, ("batch", "seq")),
            P(),
            P(None, ("batch", "seq"), None),
            P(None, ("batch", "seq"), None),
            P(None, ("batch", "seq")),
            P(None, ("batch", "seq")),
            P(),
            P(),
            P("batch"),
        ),
        out_specs=(
            P("batch", "seq", None),
            P("batch", "seq", None),
            P(),
            P(None, ("batch", "seq"), None),
            P(None, ("batch", "seq"), None),
            P(None, ("batch", "seq"), None),
            P(None, ("batch", "seq")),
            P(None, ("batch", "seq")),
            P(None, ("batch", "seq")),
            P(),
            P(),
            P(),
            P(),
        ),
        check_vma=False,
    )
```

profile of v0, /device:TPU:0, one launch (start us, length us, event | category | flops | bytes accessed | tf_op | source)
XLA Modules:
  0.0 1619.3 jit_solution(9130430659650695333)
XLA Ops:
  10.3 43.2 %all-gather.2 = bf16[32,40,2]{1,2,0:T(2,128)(2,1)S(1)} all-gather(bf16[1,40,2]{1,2,0:T(2,128)(2,1)S(1)} %convert_bitcast_fusion), channel_id=1, replica_groups=mesh['batch'=4,'seq'=8] {'batch','seq'}, dimensions={0}, use_global_device_ids=true | all-gather | bytes 5280 | tf_op jit(solution)/shard_map/all_gather | solution.py:96
  54.5 87.7 %all-gather.7.cloned.1.call-done = bf16[6,1280,1280]{2,1,0:T(8,128)(2,1)} async-done(((bf16[6,40,1280]{2,1,0:T(8,128)(2,1)}), bf16[6,1280,1280]{2,1,0:T(8,128)(2,1)}) %all-gather.7.cloned.1.call-update) | async-done | bytes 19660816 | tf_op jit(solution)/shard_map/all_gather | solution.py:95
  142.3 11.3 fusion.75
  159.4 93.6 %all-gather.9.cloned.1.call-done = bf16[1,2,2048,1280]{3,2,0,1:T(8,128)(2,1)} async-done(((bf16[1,2,256,1280]{3,2,0,1:T(8,128)(2,1)}), bf16[1,2,2048,1280]{3,2,0,1:T(8,128)(2,1)}) %all-gather.9.cloned.1.call-update) | async-done | bytes 10485776 | tf_op jit(solution)/shard_map/all_gather | solution.py:110
  253.0 14.7 copy.130
  267.6 85.3 %all-gather.11.cloned.1.call-done = bf16[1,2,2048,1280]{3,2,0,1:T(8,128)(2,1)} async-done(((bf16[1,2,256,1280]{3,2,0,1:T(8,128)(2,1)}), bf16[1,2,2048,1280]{3,2,0,1:T(8,128)(2,1)}) %all-gather.11.cloned.1.call-update) | async-done | bytes 10485776 | tf_op jit(solution)/shard_map/all_gather | solution.py:111
  353.0 14.4 copy.131
  367.4 93.7 %while.63 = (s32[]{:T(128)}, bf16[2,256,1280]{1,2,0:T(8,128)(2,1)}, f32[2,256,16]{1,2,0:T(8,128)S(1)}, bf16[2,256,1280]{1,2,0:T(8,128)(2,1)S(1)}, bf16[2,2048,12...) while((s32[]{:T(128)}, bf16[2,256,1280]{1,2,0:T(8,128)(2,1)}, ...), condition=%wide.region_6.7_spmd.clone.clone, body=%wide.region_1.6_spmd.clone.clone.sunk | while | flops 688924928 | bytes 59849560 | solution.py:142
  367.4 10.2 constant_dynamic-slice_fusion.29
  378.2 34.9 %while.66 = (s32[]{:T(128)}, bf16[4,256,320]{1,2,0:T(8,128)(2,1)S(1)}, f32[4,256,4]{1,2,0:T(4,128)S(1)}, bf16[4,2048,320]{1,2,0:T(8,128)(2,1)}, s32[2048]{0:T(10...) while((s32[]{:T(128)}, ...), condition=%wide.region_5.5_spmd.clone, body=%wide.region_2.4_spmd.clone.sunk | while | flops 688924672 | bytes 36181112 | solution.py:132
  414.2 10.2 constant_dynamic-slice_fusion.29
  425.0 34.9 %while.66 = (s32[]{:T(128)}, bf16[4,256,320]{1,2,0:T(8,128)(2,1)S(1)}, f32[4,256,4]{1,2,0:T(4,128)S(1)}, bf16[4,2048,320]{1,2,0:T(8,128)(2,1)}, s32[2048]{0:T(10...) while((s32[]{:T(128)}, ...), condition=%wide.region_5.5_spmd.clone, body=%wide.region_2.4_spmd.clone.sunk | while | flops 688924672 | bytes 36181112 | solution.py:132
  485.8 209.1 %while.65 = (s32[]{:T(128)}, bf16[2,256,1280]{2,1,0:T(8,128)(2,1)}, bf16[2,2048,1280]{2,1,0:T(8,128)(2,1)}, bf16[2,2048,1280]{2,1,0:T(8,128)(2,1)}, bf16[2,256,1...) while((s32[]{:T(128)}, bf16[2,256,1280]{2,1,0:T(8,128)(2,1)}, ...), condition=%wide.region_13.14_spmd.clone.clone, body=%wide.region_9.13_spmd.clone.clone.sunk | while | flops 1703937280 | bytes 200634352 | solution.py:258
  497.4 67.5 %while.67 = (s32[]{:T(128)}, bf16[4,256,320]{1,2,0:T(8,128)(2,1)S(1)}, bf16[4,2048,320]{1,2,0:T(8,128)(2,1)}, bf16[4,2048,320]{1,2,0:T(8,128)(2,1)}, bf16[4,2048...) while((s32[]{:T(128)}, ...), condition=%wide.region_12.12_spmd.clone, body=%wide.region_10.11_spmd.clone.sunk | while | flops 1703937024 | bytes 83904152 | solution.py:253
  601.6 67.5 %while.67 = (s32[]{:T(128)}, bf16[4,256,320]{1,2,0:T(8,128)(2,1)S(1)}, bf16[4,2048,320]{1,2,0:T(8,128)(2,1)}, bf16[4,2048,320]{1,2,0:T(8,128)(2,1)}, bf16[4,2048...) while((s32[]{:T(128)}, ...), condition=%wide.region_12.12_spmd.clone, body=%wide.region_10.11_spmd.clone.sunk | while | flops 1703937024 | bytes 83904152 | solution.py:253
  714.1 88.9 %reduce-scatter.5.cloned.1.call-done = bf16[2,256,1280]{2,1,0:T(8,128)(2,1)} async-done(((bf16[2,2048,1280]{2,1,0:T(8,128)(2,1)}), bf16[2,256,1280]{2,1,0:T(8,128)(2,1)}) %reduce-scatter.5.cloned.1.call-update) | async-done | bytes 1310736 | tf_op jit(solution)/shard_map/reduce_scatter | solution.py:262
  802.9 110.0 %reduce-scatter.7.cloned.1.call-done = bf16[2,256,1280]{2,1,0:T(8,128)(2,1)} async-done(((bf16[2,2048,1280]{2,1,0:T(8,128)(2,1)}), bf16[2,256,1280]{2,1,0:T(8,128)(2,1)}) %reduce-scatter.7.cloned.1.call-update) | async-done | bytes 1310736 | tf_op jit(solution)/shard_map/reduce_scatter | solution.py:265
  912.9 13.0 convolution_bitcast_fusion
  926.0 21.7 %pad_maximum_fusion = f32[6,1280,1280]{1,2,0:T(8,128)} fusion(f32[1,1280,1280]{1,2,0:T(8,128)S(1)} %copy-done.8, f32[1,1280,1280]{1,2,0:T(8,128)S(1)} %copy-done.1, f32[1,1280,1280]{1,2,0:T(8,128)S(1)} %bitcast.285, f32[3,1280,1280]{1,2,0:T(8,128)} %convolution_bitcast_fusion), kind=kLoop, calls=%fused_computation.59 | loop fusion | flops 29491200 | bytes 78643200 | tf_op jit(solution)/shard_map/concatenate | solution.py:287
  947.6 53.9 %copy.146 = f32[6,1280,1280]{2,0,1:T(8,128)} copy(f32[6,1280,1280]{1,2,0:T(8,128)} %pad_maximum_fusion) | data formatting | bytes 78643200 | tf_op jit(solution)/shard_map/concatenate | solution.py:287
  1004.3 13.5 fusion.52
  1017.9 40.1 %all-reduce.2 = (f32[2,1280]{1,0:T(2,128)S(1)}, f32[80]{0:T(128)S(1)}) all-reduce(f32[2,1280]{1,0:T(2,128)S(1)} %pad_maximum_fusion.4, f32[80]{0:T(128)S(1)} %multiply_multiply_fusion.3), channel_id=7, replica_groups=mesh['batch'=4,'seq'=8] {'batch','seq'}, use_global_device_ids=true, to_apply=%region_21.22.clone | all-reduce | flops 2640 | bytes 21120
  1060.0 498.4 %reduce-scatter.9.cloned.1.call-done = f32[6,40,1280]{2,0,1:T(8,128)} async-done(((f32[6,1280,1280]{2,0,1:T(8,128)}), f32[6,40,1280]{2,0,1:T(8,128)}) %reduce-scatter.9.cloned.1.call-update) | async-done | bytes 1228816 | tf_op jit(solution)/shard_map/reduce_scatter | solution.py:292
  1566.5 36.8 %all-reduce.1 = (f32[]{:T(128)}, f32[3]{0:T(128)S(1)}) all-reduce(f32[]{:T(128)S(6)} %add.149, f32[3]{0:T(128)S(1)} %pad_maximum_fusion.5), channel_id=1, replica_groups=mesh['batch'=4,'seq'=8] {'batch','seq'}, use_global_device_ids=true, to_apply=%region_27.28 | all-reduce | flops 4 | bytes 32 | tf_op jit(solution)/shard_map/psum | solution.py:299
  (406 shorter events, 351.8 us)
Async XLA Ops:
  7.2 47.0 %copy-start.9 = (bf16[2,256,1280]{2,1,0:T(8,128)(2,1)S(1)}, bf16[2,256,1280]{2,1,0:T(8,128)(2,1)}, u32[]{:S(2)}) copy-start(bf16[2,256,1280]{2,1,0:T(8,128)(2,1)} %param.20) | copy-start | bytes 3932164
  7.2 135.1 %all-gather.7.cloned.1.call-start = ((), (), s32[]{:S(2)}) async-start(), calls=%async_computation.3 | async-start | bytes 20275200 | tf_op jit(solution)/shard_map/all_gather | solution.py:95
  9.5 243.4 %all-gather.9.cloned.1.call-start = ((), (), s32[]{:S(2)}) async-start(), calls=%async_computation.7 | async-start | bytes 11796480 | tf_op jit(solution)/shard_map/all_gather | solution.py:110
  54.2 99.4 %copy-start.22 = (f32[1280]{0:T(1024)}, f32[1280]{0:T(1024)S(1)}, u32[]{:S(2)}) copy-start(f32[1280]{0:T(1024)S(1)} %get-tuple-element.566) | copy-start | bytes 15364
  54.5 99.1 %copy-start.24 = (f32[2,256]{1,0:T(2,128)}, f32[2,256]{1,0:T(2,128)S(1)}, u32[]{:S(2)}) copy-start(f32[2,256]{1,0:T(2,128)S(1)} %add_rsqrt_fusion.1) | copy-start | bytes 6148
  155.3 197.7 %all-gather.11.cloned.1.call-start = ((), (), s32[]{:S(2)}) async-start(), calls=%async_computation.8 | async-start | bytes 11796480 | tf_op jit(solution)/shard_map/all_gather | solution.py:111
  156.0 646.9 %reduce-scatter.5.cloned.1.call-start = ((), (), s32[]{:S(2)}) async-start(), calls=%async_computation.4 | async-start | bytes 11796480 | tf_op jit(solution)/shard_map/reduce_scatter | solution.py:262
  353.0 14.4 copy-start.35
  466.8 15.4 copy-start.5
  466.8 15.4 copy-start.20
  695.0 217.9 %reduce-scatter.7.cloned.1.call-start = ((), (), s32[]{:S(2)}) async-start(), calls=%async_computation.5 | async-start | bytes 11796480 | tf_op jit(solution)/shard_map/reduce_scatter | solution.py:265
  695.6 862.8 %reduce-scatter.9.cloned.1.call-start = ((), (), s32[]{:S(2)}) async-start(), calls=%async_computation.6 | async-start | bytes 54067200 | tf_op jit(solution)/shard_map/reduce_scatter | solution.py:292
  709.3 203.6 %copy-start.23 = (f32[1280]{0:T(1024)S(1)}, f32[1280]{0:T(1024)}, u32[]{:S(2)}) copy-start(f32[1280]{0:T(1024)} %copy-done.22) | copy-start | bytes 15364
  709.3 203.6 %copy-start.25 = (f32[2,256]{1,0:T(2,128)S(1)}, f32[2,256]{1,0:T(2,128)}, u32[]{:S(2)}) copy-start(f32[2,256]{1,0:T(2,128)} %copy-done.24) | copy-start | bytes 6148
  709.3 216.6 %slice-start = ((s8[6553600]{0:T(1024)(128)(4,1)}), s8[2359296]{0:T(1024)(128)(4,1)S(1)}, s32[]{:S(2)}) async-start(s8[6553600]{0:T(1024)(128)(4,1)} %bitcast.284), calls=%async_computation.9 | async-start | bytes 4718592
  912.9 13.1 slice-start.1
  912.9 13.1 copy-start.1
  912.9 13.1 copy-start.8
  1004.3 557.8 %copy-start.4 = (f32[2,256,1280]{2,1,0:T(8,128)S(1)}, f32[2,256,1280]{2,1,0:T(8,128)}, u32[]{:S(2)}) copy-start(f32[2,256,1280]{2,1,0:T(8,128)} %copy-done.2) | copy-start | bytes 7864324
  1562.2 42.5 %copy-start.32 = (f32[80]{0:T(128)S(1)}, f32[80]{0:T(128)}, u32[]{:S(2)}) copy-start(f32[80]{0:T(128)} %param.29) | copy-start | bytes 964
  1562.2 42.4 %copy-start.33 = (f32[80]{0:T(128)S(1)}, f32[80]{0:T(128)}, u32[]{:S(2)}) copy-start(f32[80]{0:T(128)} %param.30) | copy-start | bytes 964
  1562.2 43.0 %copy-start.27 = (f32[2,40]{1,0:T(2,128)S(1)}, f32[2,40]{1,0:T(2,128)}, u32[]{:S(2)}) copy-start(f32[2,40]{1,0:T(2,128)} %param.23) | copy-start | bytes 964
  1562.2 43.0 %copy-start.28 = (f32[2,40]{1,0:T(2,128)S(1)}, f32[2,40]{1,0:T(2,128)}, u32[]{:S(2)}) copy-start(f32[2,40]{1,0:T(2,128)} %param.27) | copy-start | bytes 964
  1562.2 43.0 %copy-start.29 = (f32[2,40]{1,0:T(2,128)S(1)}, f32[2,40]{1,0:T(2,128)}, u32[]{:S(2)}) copy-start(f32[2,40]{1,0:T(2,128)} %param.28) | copy-start | bytes 964
  (24 other events, 95.3 us)
Sparse Core Ops, SparseCore 0:
  11.5 130.7 all-gather.6
  155.4 97.5 all-gather.8
  255.2 97.7 all-gather.10
  695.1 107.7 reduce-scatter.4
  805.1 107.7 reduce-scatter.6
  1001.7 556.6 reduce-scatter.8
where the time goes:
time: 1630 us; the launch traced here: 1620 us
  waiting for transfers between devices  965 us (59%)
  local copies, waits for them, and re-layouts  238 us (15%)
  matrix products  175 us (11%)
  blocking collectives  120 us (7%)
  other arithmetic  100 us (6%)
  between operations  18.6 us (1%)
    reduce_scatter x1, waiting for transfers between devices, body(): lax.psum_scatter(weight_grads, ('batch', 'seq'), scatter_dimension=1, til...  498 us
    reduce_scatter x1, waiting for transfers between devices, body(): lax.psum_scatter(values_parts.astype(jnp.bfloat16), 'seq', scatter_dimens...  110 us
    all_gather x1, waiting for transfers between devices, body(): lax.all_gather(keys_own, 'seq', axis=1, tiled=True)  93.6 us
    reduce_scatter x1, waiting for transfers between devices, body(): lax.psum_scatter(keys_parts.astype(jnp.bfloat16), 'seq', scatter_dimensio...  88.9 us
    all_gather x1, waiting for transfers between devices, body(): lax.all_gather(low_weights, ('batch', 'seq'), axis=1, tiled=True)  87.7 us
    all_gather x1, waiting for transfers between devices, body(): lax.all_gather(values_own, 'seq', axis=1, tiled=True)  85.3 us
    concatenate x1, local copies, waits for them, and re-layouts, body(): jnp.concatenate([grad_inner, jnp.stack([grad_out_proj, grad_up, grad_down...  53.9 us
    dynamic_update_slice x6, local copies, waits for them, and re-layouts, body(): lax.map(query_full, (queries, grad_attended, log_totals, all_keys, all_va...  48.9 us
  transfers between devices with their start and end apart: 6, of which 6 were waited for; matrix products, arithmetic and copies ran while one was open for 3% of the time, Pallas kernels for 0%

commit v1 on v0

v1 whole, which is shorter than its diff:
```python
import functools
import math

import jax
import jax.numpy as jnp
from jax import lax
from jax.experimental import pallas as pl
from jax.experimental.pallas import tpu as pltpu
from jax.sharding import PartitionSpec as P

STEP = 10

NORM_EPS = 1e-06
LOG_TWO_E = 1.442695
BETA_FIRST = 0.9
BETA_SECOND = 0.999
ADAM_EPS = 1e-08
MATRIX_RATE = 0.05
GAIN_RATE = 0.5
MATRIX_DECAY = 0.1
CLIP_NORM = 1.0
MASKED = -1e30

MESH = pl.DeviceIdType.MESH
LANES = 128
F32 = jnp.float32
LOW = jnp.bfloat16
MIB = 1024 * 1024


def rms_factor(values):
    return lax.rsqrt(jnp.mean(values * values, axis=-1, keepdims=True) + NORM_EPS)


def norm_back(grad_normed, normed, factor):
    return factor * (grad_normed - normed * jnp.mean(grad_normed * normed, axis=-1, keepdims=True))


def silu_slope(values):
    logistic = jax.nn.sigmoid(values)
    return logistic * (1.0 + values * (1.0 - logistic))


def adam_update(current, gradient, moment_one, moment_two, step_rate, decay_rate):
    new_one = BETA_FIRST * moment_one + (1.0 - BETA_FIRST) * gradient
    new_two = BETA_SECOND * moment_two + (1.0 - BETA_SECOND) * gradient * gradient
    first_hat = new_one / (1.0 - BETA_FIRST**STEP)
    second_hat = new_two / (1.0 - BETA_SECOND**STEP)
    updated = current - step_rate * (
        first_hat / (jnp.sqrt(second_hat) + ADAM_EPS) + decay_rate * current
    )
    return (updated, new_one, new_two)


def dot(left, right, left_axis=1, right_axis=0):
    return lax.dot_general(
        left, right, (((left_axis,), (right_axis,)), ((), ())), preferred_element_type=F32
    )


def greet(seq_count, batch_count):
    barrier = pltpu.get_barrier_semaphore()
    me_seq, me_batch = lax.axis_index("seq"), lax.axis_index("batch")
    for k in range(1, seq_count):
        pl.semaphore_signal(
            barrier,
            inc=1,
            device_id={"seq": lax.rem(me_seq + k, seq_count)},
            device_id_type=MESH,
        )
    for k in range(1, batch_count):
        pl.semaphore_signal(
            barrier,
            inc=1,
            device_id={"batch": lax.rem(me_batch + k, batch_count)},
            device_id_type=MESH,
        )
    pl.semaphore_wait(barrier, seq_count - 1 + batch_count - 1)


def push(source, target, send_sem, recv_sem, **where):
    return pltpu.make_async_remote_copy(
        source, target, send_sem, recv_sem, device_id=where, device_id_type=MESH
    )


def place(seq_count):
    me = lax.axis_index("seq")
    chips = seq_count // 2
    half_chips = chips // 2
    core = lax.rem(me, 2)
    chip = me // 2
    half = chip // half_chips
    base = half * half_chips
    gate_mine = half_chips - 1 + half
    gate_other = half_chips - half
    return me, core, chip, half, base, gate_mine, gate_other


def far_chip(step, half, half_chips):
    return (1 - half) * (half_chips + step) + half * (half_chips - 1 - step)


def gather_kernel(
    n, nb, chunks, tok, slab, xg, wout, far_sem, own_sem, pass_sem, sib_sem, same_recv, sib_recv,
    z_send, z_recv, b_send, b_recv, local_sem,
):
    chips, half_chips = n // 2, n // 4
    me, core, chip, half, base, gate_mine, gate_other = place(n)
    group_count = n // 2
    batch = lax.axis_index("batch")
    rows = tok.shape[1] // chunks
    sibling = 2 * chip + 1 - core
    greet(n, nb)

    z_copies = []
    for k in range(1, n):
        target = lax.rem(me + k, n)
        copy = push(
            slab.at[lax.rem(target, group_count)], wout.at[batch, me], z_send.at[k],
            z_recv.at[k], seq=target,
        )
        copy.start()
        z_copies.append(copy)

    def part(ref, lead, c):
        return ref.at[lead, pl.ds(c * rows, rows)]

    def tok_copy(source, slot, c, send_sem, recv_sem, target):
        return push(source, part(xg, slot, c), send_sem, recv_sem.at[slot, c], seq=target)

    sends = []
    for c in range(chunks):
        copy = tok_copy(
            part(tok, 1 - half, c), me, c, far_sem.at[c], same_recv, 2 * gate_other + core
        )
        copy.start()
        sends.append(copy)
        for k in range(1, half_chips):
            other = base + lax.rem(chip - base + k, half_chips)
            copy = tok_copy(
                part(tok, half, c), me, c, own_sem.at[k, c], same_recv, 2 * other + core
            )
            copy.start()
            sends.append(copy)
        copy = tok_copy(part(tok, half, c), me, c, sib_sem.at[0, c], sib_recv, sibling)
        copy.start()
        sends.append(copy)
    own_copy = pltpu.make_async_copy(tok.at[half], xg.at[me], local_sem.at[0])
    own_copy.start()
    slab_copy = pltpu.make_async_copy(
        slab.at[lax.rem(me, group_count)], wout.at[batch, me], local_sem.at[1]
    )
    slab_copy.start()
    slab_copy.wait()

    b_copies = []

    def spread(source, index):
        for j in range(1, nb):
            copy = push(
                wout.at[batch, source], wout.at[batch, source], b_send.at[j, index],
                b_recv.at[j, index], batch=lax.rem(batch + j, nb),
            )
            copy.start()
            b_copies.append(copy)

    spread(me, 0)
    for k in range(1, n):
        z_copies[k - 1].wait_recv()
        spread(lax.rem(me + n - k, n), k)

    for c in range(chunks):
        for k in range(1, half_chips):
            slot = 2 * (base + lax.rem(chip - base + half_chips - k, half_chips)) + core
            arrived = tok_copy(part(xg, slot, c), slot, c, sib_sem.at[k, c], same_recv, sibling)
            arrived.wait_recv()
            copy = tok_copy(part(xg, slot, c), slot, c, sib_sem.at[k, c], sib_recv, sibling)
            copy.start()
            sends.append(copy)
        for k in range(half_chips):
            slot = 2 * far_chip(k, half, half_chips) + core
            lane = half_chips + k
            tok_copy(part(xg, slot, c), slot, c, sib_sem.at[lane, c], same_recv, sibling).wait_recv()

            @pl.when(chip == gate_mine)
            def _():
                for j in range(1, half_chips):
                    other = base + lax.rem(chip - base + j, half_chips)
                    tok_copy(
                        part(xg, slot, c), slot, c, pass_sem.at[k, j, c], same_recv,
                        2 * other + core,
                    ).start()

            copy = tok_copy(part(xg, slot, c), slot, c, sib_sem.at[lane, c], sib_recv, sibling)
            copy.start()
            sends.append(copy)

    for c in range(chunks):
        for q in range(chips):
            slot = 2 * q + 1 - core
            tok_copy(part(xg, slot, c), slot, c, sib_sem.at[0, c], sib_recv, sibling).wait_recv()
    own_copy.wait()
    for copy in b_copies:
        copy.wait_recv()
    for copy in sends + b_copies + z_copies:
        copy.wait_send()

    @pl.when(chip == gate_mine)
    def _():
        for c in range(chunks):
            for k in range(half_chips):
                for j in range(1, half_chips):
                    tok_copy(
                        part(xg, me, c), me, c, pass_sem.at[k, j, c], same_recv, sibling
                    ).wait_send()


def gather_tokens(n, nb, tokens, slab):
    chunks = 4
    chips, half_chips = n // 2, n // 4
    dma = pltpu.SemaphoreType.DMA
    return pl.pallas_call(
        functools.partial(gather_kernel, n, nb, chunks),
        out_shape=(
            jax.ShapeDtypeStruct((n,) + tokens.shape[1:], tokens.dtype),
            jax.ShapeDtypeStruct((nb, n) + slab.shape[1:], slab.dtype),
        ),
        in_specs=[pl.BlockSpec(memory_space=pl.ANY)] * 2,
        out_specs=[pl.BlockSpec(memory_space=pl.ANY)] * 2,
        scratch_shapes=[
            dma((chunks,)),
            dma((half_chips, chunks)),
            dma((half_chips, half_chips, chunks)),
            dma((chips, chunks)),
            dma((n, chunks)),
            dma((n, chunks)),
            dma((n,)),
            dma((n,)),
            dma((nb, n)),
            dma((nb, n)),
            dma((2,)),
        ],
        compiler_params=pltpu.CompilerParams(collective_id=1, has_side_effects=True),
        name="gather_tokens",
    )(tokens, slab)


def swap_kernel(n, source, target, send_sem, recv_sem, local_sem):
    me = lax.axis_index("seq")
    greet(n, 1)
    copies = []
    for k in range(1, n):
        other = lax.rem(me + k, n)
        copy = push(source.at[other], target.at[me], send_sem.at[k], recv_sem.at[k], seq=other)
        copy.start()
        copies.append(copy)
    own = pltpu.make_async_copy(source.at[me], target.at[me], local_sem)
    own.start()
    own.wait()
    for copy in copies:
        copy.wait()


def swap_blocks(n, blocks, collective_id):
    return pl.pallas_call(
        functools.partial(swap_kernel, n),
        out_shape=jax.ShapeDtypeStruct(blocks.shape, blocks.dtype),
        in_specs=[pl.BlockSpec(memory_space=pl.ANY)],
        out_specs=pl.BlockSpec(memory_space=pl.ANY),
        scratch_shapes=[
            pltpu.SemaphoreType.DMA((n,)),
            pltpu.SemaphoreType.DMA((n,)),
            pltpu.SemaphoreType.DMA,
        ],
        compiler_params=pltpu.CompilerParams(collective_id=collective_id, has_side_effects=True),
        name="swap_blocks",
    )(blocks)


def widen(values):
    rows, width = values.shape
    return jnp.concatenate([values, jnp.zeros((rows, LANES - width), values.dtype)], axis=1)


def project_kernel(heads, size, x_ref, w_ref, gain_ref, coef_ref, h_ref, qkv_ref, q_ref):
    x = x_ref[0].astype(F32)
    normed = x * rms_factor(x)
    h = (normed * gain_ref[...]).astype(LOW)
    h_ref[0] = h
    out = dot(h, w_ref[...])
    for a in range(heads):
        q = widen(out[:, a * size : (a + 1) * size])
        q_ref[a] = q
        qkv_ref[a] = (q * coef_ref[...]).astype(LOW)
    for a in range(heads, 3 * heads):
        qkv_ref[a] = widen(out[:, a * size : (a + 1) * size].astype(LOW))


def project(heads, size, xg, weights, gain, coef):
    n, rows, width = xg.shape
    return pl.pallas_call(
        functools.partial(project_kernel, heads, size),
        grid=(n,),
        out_shape=(
            jax.ShapeDtypeStruct(xg.shape, LOW),
            jax.ShapeDtypeStruct((3 * heads, n * rows, LANES), LOW),
            jax.ShapeDtypeStruct((heads, n * rows, LANES), F32),
        ),
        in_specs=[
            pl.BlockSpec((1, rows, width), lambda i: (i, 0, 0)),
            pl.BlockSpec(weights.shape, lambda i: (0, 0)),
            pl.BlockSpec(gain.shape, lambda i: (0, 0)),
            pl.BlockSpec(coef.shape, lambda i: (0, 0)),
        ],
        out_specs=[
            pl.BlockSpec((1, rows, width), lambda i: (i, 0, 0)),
            pl.BlockSpec((3 * heads, rows, LANES), lambda i: (0, i, 0)),
            pl.BlockSpec((heads, rows, LANES), lambda i: (0, i, 0)),
        ],
        compiler_params=pltpu.CompilerParams(vmem_limit_bytes=48 * MIB),
        name="project",
    )(xg, weights, gain, coef)


def attend_kernel(
    heads, size, fold, len_ref, q_ref, k_ref, v_ref, o_ref, keep_ref, lse_ref, s_ref, m_ref, acc_ref,
    sum_ref,
):
    i = pl.program_id(0)
    block = q_ref.shape[1]
    length = len_ref[0]
    whole = jnp.minimum(i, length // block)
    total = jnp.minimum(i + 1, pl.cdiv(length, block))
    m_ref[...] = jnp.full_like(m_ref, MASKED)
    sum_ref[...] = jnp.zeros_like(sum_ref)
    acc_ref[...] = jnp.zeros_like(acc_ref)

    def score(j, masked):
        keys = pl.ds(pl.multiple_of(j * block, block), block)
        if masked:
            row = i * block + lax.broadcasted_iota(jnp.int32, (block, block), 0)
            col = j * block + lax.broadcasted_iota(jnp.int32, (block, block), 1)
            visible = (col <= row) & (col < length)
        for a in range(heads):
            s = dot(q_ref[a], k_ref[a, keys], 1, 1)
            if masked:
                s = jnp.where(visible, s, MASKED)
            s_ref[a, j] = s
            best = m_ref[a]
            for part in range(block // LANES):
                best = jnp.maximum(best, s[:, part * LANES : (part + 1) * LANES])
            m_ref[a] = best

    pl.loop(0, whole)(lambda j: score(j, False))
    pl.loop(whole, total)(lambda j: score(j, True))
    for a in range(heads):
        m_ref[a] = jnp.broadcast_to(jnp.max(m_ref[a], axis=1, keepdims=True), (block, LANES))

    @pl.loop(0, total)
    def _(j):
        keys = pl.ds(pl.multiple_of(j * block, block), block)
        for a in range(heads):
            best = m_ref[a]
            count = sum_ref[a]
            pieces = []
            for part in range(block // LANES):
                e = jnp.exp(s_ref[a, j, :, part * LANES : (part + 1) * LANES] - best)
                count = count + e
                pieces.append(e.astype(LOW))
            sum_ref[a] = count
            acc_ref[a] += dot(jnp.concatenate(pieces, axis=1), v_ref[a, keys])

    outs = []
    for a in range(heads):
        count = jnp.sum(sum_ref[a], axis=1, keepdims=True)
        out = acc_ref[a] / count
        keep_ref[a] = out
        outs.append(out[:, :size])
        lse = m_ref[a] + jnp.log(count)
        lse_ref[a] = lse.T[:8]
    low = jnp.concatenate(outs, axis=1).astype(LOW)
    piece = block // fold
    o_ref[0] = jnp.concatenate([low[f * piece : (f + 1) * piece] for f in range(fold)], axis=1)


def attend(heads, size, fold, length, qkv, n):
    full = qkv.shape[1]
    block = full // n
    width = heads * size * fold
    return pl.pallas_call(
        functools.partial(attend_kernel, heads, size, fold),
        grid=(n,),
        out_shape=(
            jax.ShapeDtypeStruct((n, block // fold, width), LOW),
            jax.ShapeDtypeStruct((heads, full, LANES), F32),
            jax.ShapeDtypeStruct((heads, 8, full), F32),
        ),
        in_specs=[
            pl.BlockSpec(memory_space=pltpu.SMEM),
            pl.BlockSpec((heads, block, LANES), lambda i: (0, i, 0)),
            pl.BlockSpec((heads, full, LANES), lambda i: (1, 0, 0)),
            pl.BlockSpec((heads, full, LANES), lambda i: (2, 0, 0)),
        ],
        out_specs=[
            pl.BlockSpec((1, block // fold, width), lambda i: (i, 0, 0)),
            pl.BlockSpec((heads, block, LANES), lambda i: (0, i, 0)),
            pl.BlockSpec((heads, 8, block), lambda i: (0, 0, i)),
        ],
        scratch_shapes=[
            pltpu.VMEM((heads, n, block, block), F32),
            pltpu.VMEM((heads, block, LANES), F32),
            pltpu.VMEM((heads, block, LANES), F32),
            pltpu.VMEM((heads, block, LANES), F32),
        ],
        compiler_params=pltpu.CompilerParams(vmem_limit_bytes=48 * MIB),
        name="attend",
    )(length, qkv, qkv, qkv)


def attend_back_kernel(
    heads, size, fold, n, len_ref, coef_ref, q_ref, k_ref, v_ref, go_ref, keep_ref, lse_ref, qf_ref,
    out_ref, scale_ref, kt_ref, gq_ref, gqt_ref, gk_ref, gv_ref, g_ref, delta_ref,
):
    i = pl.program_id(0)
    block = q_ref.shape[1]
    length = len_ref[0]
    whole = jnp.minimum(i, length // block)
    total = jnp.minimum(i + 1, pl.cdiv(length, block))

    @pl.when(i == 0)
    def _():
        gk_ref[...] = jnp.zeros_like(gk_ref)
        gv_ref[...] = jnp.zeros_like(gv_ref)
        scale_ref[...] = jnp.zeros_like(scale_ref)

        @pl.loop(0, n)
        def _(j):
            keys = pl.ds(pl.multiple_of(j * block, block), block)
            for a in range(heads):
                kt_ref[a, j] = k_ref[a, keys].T

    gqt_ref[...] = jnp.zeros_like(gqt_ref)
    for a in range(heads):
        g = widen(
            jnp.concatenate(
                [
                    go_ref[0, :, (f * heads + a) * size : (f * heads + a + 1) * size]
                    for f in range(fold)
                ],
                axis=0,
            )
        )
        g_ref[a] = g
        delta_ref[a] = jnp.broadcast_to(
            jnp.sum((g.astype(F32) * keep_ref[a]).T, axis=0, keepdims=True), (8, block)
        )

    def back(j, masked):
        keys = pl.ds(pl.multiple_of(j * block, block), block)
        if masked:
            col = j * block + lax.broadcasted_iota(jnp.int32, (block, block), 0)
            row = i * block + lax.broadcasted_iota(jnp.int32, (block, block), 1)
            visible = (col <= row) & (col < length)
        for a in range(heads):
            s = dot(k_ref[a, keys], q_ref[a], 1, 1)
            p = jnp.exp(s - lse_ref[a, :1])
            if masked:
                p = jnp.where(visible, p, 0.0)
            dp = dot(v_ref[a, keys], g_ref[a], 1, 1)
            ds = (p * (dp - delta_ref[a, :1])).astype(LOW)
            gk_ref[a, keys] += dot(ds, q_ref[a])
            gv_ref[a, keys] += dot(p.astype(LOW), g_ref[a])
            gqt_ref[a] += dot(kt_ref[a, j], ds)

    pl.loop(0, whole)(lambda j: back(j, False))
    pl.loop(whole, total)(lambda j: back(j, True))

    rows = pl.ds(pl.multiple_of(i * block, block), block)
    for a in range(heads):
        grad = gqt_ref[a].T.astype(LOW).astype(F32)
        scale_ref[...] += jnp.sum((grad * qf_ref[a]).reshape(block // 8, 8, LANES), axis=0)
        gq_ref[a, rows] = (grad * coef_ref[...]).astype(LOW)

    @pl.when(i == n - 1)
    def _():
        @pl.loop(0, n)
        def _(j):
            keys = pl.ds(pl.multiple_of(j * block, block), block)
            pieces = [gq_ref[a, keys][:, :size] for a in range(heads)]
            pieces += [gk_ref[a, keys][:, :size].astype(LOW) for a in range(heads)]
            pieces += [gv_ref[a, keys][:, :size].astype(LOW) for a in range(heads)]
            spare = out_ref.shape[2] - 3 * heads * size
            pieces.append(jnp.zeros((block, spare), LOW))
            out_ref[j] = jnp.concatenate(pieces, axis=1)


def attend_back(heads, size, fold, length, coef, qkv, go, keep, lse, q_full, n, slab_width):
    full = qkv.shape[1]
    block = full // n
    width = heads * size * fold
    return pl.pallas_call(
        functools.partial(attend_back_kernel, heads, size, fold, n),
        grid=(n,),
        out_shape=(
            jax.ShapeDtypeStruct((n, block, slab_width), LOW),
            jax.ShapeDtypeStruct((8, LANES), F32),
        ),
        in_specs=[
            pl.BlockSpec(memory_space=pltpu.SMEM),
            pl.BlockSpec(coef.shape, lambda i: (0, 0)),
            pl.BlockSpec((heads, block, LANES), lambda i: (0, i, 0)),
            pl.BlockSpec((heads, full, LANES), lambda i: (1, 0, 0)),
            pl.BlockSpec((heads, full, LANES), lambda i: (2, 0, 0)),
            pl.BlockSpec((1, block // fold, width), lambda i: (i, 0, 0)),
            pl.BlockSpec((heads, block, LANES), lambda i: (0, i, 0)),
            pl.BlockSpec((heads, 8, block), lambda i: (0, 0, i)),
            pl.BlockSpec((heads, block, LANES), lambda i: (0, i, 0)),
        ],
        out_specs=[
            pl.BlockSpec((n, block, slab_width), lambda i: (0, 0, 0)),
            pl.BlockSpec((8, LANES), lambda i: (0, 0)),
        ],
        scratch_shapes=[
            pltpu.VMEM((heads, n, LANES, block), LOW),
            pltpu.VMEM((heads, full, LANES), LOW),
            pltpu.VMEM((heads, LANES, block), F32),
            pltpu.VMEM((heads, full, LANES), F32),
            pltpu.VMEM((heads, full, LANES), F32),
            pltpu.VMEM((heads, block, LANES), LOW),
            pltpu.VMEM((heads, 8, block), F32),
        ],
        compiler_params=pltpu.CompilerParams(vmem_limit_bytes=56 * MIB),
        name="attend_back",
    )(length, coef, qkv, qkv, qkv, go, keep, lse, q_full)


def reduce_kernel(
    n, nb, chunks, gh, gw, out, own_gw, from_sib, total, gate_in, peer_in, batch_in, line_out, line_in,
    sib_send, sib_recv, gate_send, gate_recv, peer_send, peer_recv, far_send, far_recv,
    b_send, b_recv, z_send, z_recv,
):
    chips, half_chips = n // 2, n // 4
    me, core, chip, half, base, gate_mine, gate_other = place(n)
    group_count = n // 2
    batch = lax.axis_index("batch")
    rows = gh.shape[1] // chunks
    sibling = 2 * chip + 1 - core
    greet(n, nb)

    b_copies = []
    for k in range(1, nb):
        target = lax.rem(batch + k, nb)
        copy = push(gw.at[target], batch_in.at[k], b_send.at[k], b_recv.at[k], batch=target)
        copy.start()
        b_copies.append(copy)

    order = [far_chip(half_chips - 1 - k, half, half_chips) for k in range(half_chips)]
    order += [base + lax.rem(chip - base + k, half_chips) for k in range(1, half_chips)]
    order += [chip]
    sib_copies = []
    for k, q in enumerate(order):
        copy = push(
            gh.at[2 * q + 1 - core], from_sib.at[q], sib_send.at[q], sib_recv.at[q], seq=sibling
        )
        copy.start()
        sib_copies.append(copy)

    def part(ref, lead, c):
        return ref.at[lead, pl.ds(c * rows, rows)]

    def add_sibling(k):
        q = order[k]
        sib_copies[k].wait_recv()
        total[q] = (gh[2 * q + core].astype(F32) + from_sib[q].astype(F32)).astype(LOW)

    def send_peer(k):
        q = order[half_chips + k - 1]
        copy = push(
            total.at[q], peer_in.at[k], peer_send.at[k], peer_recv.at[k], seq=2 * q + core
        )
        copy.start()
        return copy

    def gate_copy(j, k, c):
        return push(
            part(total, order[k], c), gate_in.at[j, k, pl.ds(c * rows, rows)],
            gate_send.at[k, c], gate_recv.at[j, k, c], seq=2 * gate_mine + core,
        )

    def far_copy(k, c):
        return push(
            part(total, order[k], c), part(out, half, c), far_send.at[k, c], far_recv.at[c],
            seq=2 * order[k] + core,
        )

    @pl.when(chip == gate_mine)
    def _():
        for k in range(1, half_chips):
            add_sibling(half_chips + k - 1)
            send_peer(k)
        for k in range(half_chips):
            add_sibling(k)
        for k in range(half_chips):
            for c in range(chunks):
                span = pl.ds(c * rows, rows)
                value = total[order[k], span].astype(F32)
                for j in range(1, half_chips):
                    gate_copy(j, k, c).wait_recv()
                    value = value + gate_in[j, k, span].astype(F32)
                total[order[k], span] = value.astype(LOW)
                far_copy(k, c).start()

    @pl.when(chip != gate_mine)
    def _():
        after = lax.rem(chip - gate_mine + half_chips, half_chips)
        for k in range(half_chips):
            add_sibling(k)
            for c in range(chunks):
                gate_copy(after, k, c).start()
        for k in range(1, half_chips):
            add_sibling(half_chips + k - 1)
            send_peer(k)

    add_sibling(chips - 1)

    for copy in b_copies:
        copy.wait_recv()

    @pl.loop(0, n)
    def _(s):
        value = gw[batch, s].astype(F32)
        for k in range(1, nb):
            value = value + batch_in[k, s].astype(F32)
        line_out[s] = value.astype(LOW)

    z_copies = []
    for k in range(1, n):
        target = lax.rem(me + k, n)
        copy = push(line_out.at[target], line_in.at[me], z_send.at[k], z_recv.at[k], seq=target)
        copy.start()
        z_copies.append(copy)
    line_in[me] = line_out[me]

    value = total[chip].astype(F32)
    for k in range(1, half_chips):
        push(
            total.at[chip], peer_in.at[k], peer_send.at[k], peer_recv.at[k], seq=sibling
        ).wait_recv()
        value = value + peer_in[k].astype(F32)
    out[half] = value.astype(LOW)
    for c in range(chunks):
        push(
            part(total, 0, c), part(out, 1 - half, c), far_send.at[0, c], far_recv.at[c], seq=sibling
        ).wait_recv()
    for copy in z_copies:
        copy.wait_recv()
    for g in range(group_count):
        own_gw[g] = line_in[g].astype(F32) + line_in[g + group_count].astype(F32)

    for copy in b_copies + sib_copies + z_copies:
        copy.wait_send()
    for k in range(1, half_chips):
        push(
            total.at[chip], peer_in.at[k], peer_send.at[k], peer_recv.at[k], seq=sibling
        ).wait_send()

    @pl.when(chip == gate_mine)
    def _():
        for k in range(half_chips):
            for c in range(chunks):
                far_copy(k, c).wait_send()

    @pl.when(chip != gate_mine)
    def _():
        for k in range(half_chips):
            for c in range(chunks):
                gate_copy(1, k, c).wait_send()


def reduce_grads(n, nb, gh, gw):
    chunks = 4
    chips, half_chips = n // 2, n // 4
    _, rows, width = gh.shape
    slab = gw.shape[2:]
    dma = pltpu.SemaphoreType.DMA
    return pl.pallas_call(
        functools.partial(reduce_kernel, n, nb, chunks),
        out_shape=(
            jax.ShapeDtypeStruct((2, rows, width), LOW),
            jax.ShapeDtypeStruct((n // 2,) + slab, F32),
        ),
        in_specs=[pl.BlockSpec(memory_space=pltpu.VMEM)] * 2,
        out_specs=[pl.BlockSpec(memory_space=pltpu.VMEM)] * 2,
        scratch_shapes=[
            pltpu.VMEM((chips, rows, width), LOW),
            pltpu.VMEM((chips, rows, width), LOW),
            pltpu.VMEM((half_chips, half_chips, rows, width), LOW),
            pltpu.VMEM((half_chips, rows, width), LOW),
            pltpu.VMEM((nb, n) + slab, LOW),
            pltpu.VMEM((n,) + slab, LOW),
            pltpu.VMEM((n,) + slab, LOW),
            dma((chips,)),
            dma((chips,)),
            dma((half_chips, chunks)),
            dma((half_chips, half_chips, chunks)),
            dma((half_chips,)),
            dma((half_chips,)),
            dma((half_chips, chunks)),
            dma((chunks,)),
            dma((nb,)),
            dma((nb,)),
            dma((n,)),
            dma((n,)),
        ],
        compiler_params=pltpu.CompilerParams(
            collective_id=4, has_side_effects=True, vmem_limit_bytes=60 * MIB
        ),
        name="reduce_grads",
    )(gh, gw)


def total_kernel(n, nb, value, out, mine, line_in, batch_in, z_send, z_recv, b_send, b_recv):
    me, batch = lax.axis_index("seq"), lax.axis_index("batch")
    greet(n, nb)
    copies = []
    for k in range(1, n):
        copy = push(
            value, line_in.at[k], z_send.at[k], z_recv.at[k], seq=lax.rem(me + k, n)
        )
        copy.start()
        copies.append(copy)
    line_in[0] = value[...]
    for copy in copies:
        copy.wait_recv()
    part = jnp.zeros_like(value)
    for s in range(n):
        part = part + line_in[lax.rem(me - s + n, n)]
    mine[...] = part
    for k in range(1, nb):
        copy = push(
            mine, batch_in.at[k], b_send.at[k], b_recv.at[k], batch=lax.rem(batch + k, nb)
        )
        copy.start()
        copies.append(copy)
    batch_in[0] = part
    for copy in copies[n - 1 :]:
        copy.wait_recv()
    part = jnp.zeros_like(part)
    for s in range(nb):
        part = part + batch_in[lax.rem(batch - s + nb, nb)]
    out[...] = part
    for copy in copies:
        copy.wait_send()


def total_all(n, nb, value):
    dma = pltpu.SemaphoreType.DMA
    return pl.pallas_call(
        functools.partial(total_kernel, n, nb),
        out_shape=jax.ShapeDtypeStruct(value.shape, F32),
        in_specs=[pl.BlockSpec(memory_space=pltpu.VMEM)],
        out_specs=pl.BlockSpec(memory_space=pltpu.VMEM),
        scratch_shapes=[
            pltpu.VMEM(value.shape, F32),
            pltpu.VMEM((n,) + value.shape, F32),
            pltpu.VMEM((nb,) + value.shape, F32),
            dma((n,)),
            dma((n,)),
            dma((nb,)),
            dma((nb,)),
        ],
        compiler_params=pltpu.CompilerParams(collective_id=5, has_side_effects=True),
        name="total_all",
    )(value)


def body(
    n,
    nb,
    tokens,
    cotangent,
    weights,
    gains,
    query_scale,
    first_weights,
    second_weights,
    first_gains,
    second_gains,
    first_scale,
    second_scale,
    lengths,
):
    series_count, rows, width = tokens.shape
    size = query_scale.shape[0]
    group_count = n // 2
    heads = width // size // group_count
    group_width = heads * size
    fold = 640 // group_width
    shard = weights.shape[1]
    slab_width = (3 * group_width + 2 + LANES - 1) // LANES * LANES
    half = lax.axis_index("seq") // group_count
    length = lax.dynamic_slice(lengths, (half,), (1,))

    low_weights = weights.astype(LOW)
    slab = (
        low_weights[:3]
        .reshape(3, shard, group_count, group_width)
        .transpose(2, 1, 0, 3)
        .reshape(group_count, shard, 3 * group_width)
    )
    low_gains = jnp.broadcast_to(gains.astype(LOW).T[None], (group_count, shard, 2))
    spare = jnp.zeros((group_count, shard, slab_width - 3 * group_width - 2), LOW)
    slab = jnp.concatenate([slab, low_gains, spare], axis=2)
    full_weights = lax.all_gather(low_weights[3:], ("batch", "seq"), axis=1, tiled=True)

    xg, wout = gather_tokens(n, nb, tokens, slab)
    wqkv = wout.reshape(nb * n * shard, slab_width)
    gain_rows = wqkv[:, 3 * group_width : 3 * group_width + 2].astype(F32).T
    gain_one, gain_two = gain_rows[0:1], gain_rows[1]

    coef = LOG_TWO_E / math.sqrt(size) * jax.nn.softplus(query_scale)
    coef_row = jnp.concatenate([coef, jnp.zeros((LANES - size,), F32)])[None]
    normed_in, qkv, q_full = project(heads, size, xg, wqkv, gain_one, coef_row)
    o_send, o_keep, lse = attend(heads, size, fold, length, qkv, n)
    o_recv = swap_blocks(n, o_send, 2)
    attended_low = (
        o_recv.reshape(2, group_count, rows // fold, fold, group_width)
        .transpose(0, 3, 2, 1, 4)
        .reshape(2, rows, width)
    )

    inputs = tokens.astype(F32)
    factor_one = rms_factor(inputs)
    normed_one = inputs * factor_one
    branch_one = jnp.einsum("std,de->ste", attended_low, full_weights[0], preferred_element_type=F32)
    middle = inputs + branch_one
    factor_two = rms_factor(middle)
    normed_two = middle * factor_two
    hidden_in = (normed_two * gain_two).astype(LOW)
    pre_act = jnp.einsum("std,de->ste", hidden_in, full_weights[1], preferred_element_type=F32)
    activated = jax.nn.silu(pre_act).astype(LOW)
    branch_two = jnp.einsum("std,de->ste", activated, full_weights[2], preferred_element_type=F32)
    final_sum = middle + branch_two
    block_out = final_sum.astype(LOW)
    stat_terms = jnp.stack(
        [
            jnp.sum(branch_one * branch_one),
            jnp.sum(branch_two * branch_two),
            jnp.sum(final_sum * final_sum),
        ]
    )
    grad_out = cotangent.astype(F32)
    grad_down = jnp.einsum("std,ste->de", activated, cotangent, preferred_element_type=F32)
    grad_act = jnp.einsum("ste,de->std", cotangent, full_weights[2], preferred_element_type=F32)
    grad_pre = (grad_act * silu_slope(pre_act)).astype(LOW)
    grad_up = jnp.einsum("std,ste->de", hidden_in, grad_pre, preferred_element_type=F32)
    grad_hidden = jnp.einsum("ste,de->std", grad_pre, full_weights[1], preferred_element_type=F32)
    grad_gain_two = jnp.sum(grad_hidden * normed_two, axis=(0, 1))
    grad_middle = grad_out + norm_back(grad_hidden * gain_two, normed_two, factor_two)
    grad_branch = grad_middle.astype(LOW)
    grad_out_proj = jnp.einsum("std,ste->de", attended_low, grad_branch, preferred_element_type=F32)
    grad_attended = jnp.einsum(
        "ste,de->std", grad_branch, full_weights[0], preferred_element_type=F32
    ).astype(LOW)
    go_send = (
        grad_attended.reshape(2, fold, rows // fold, group_count, group_width)
        .transpose(0, 3, 2, 1, 4)
        .reshape(n, rows // fold, fold * group_width)
    )
    go_recv = swap_blocks(n, go_send, 3)
    own_three = lax.psum_scatter(
        jnp.stack([grad_out_proj, grad_up, grad_down]).astype(LOW),
        ("batch", "seq"),
        scatter_dimension=1,
        tiled=True,
    ).astype(F32)

    grad_proj, scale_part = attend_back(
        heads, size, fold, length, coef_row, qkv, go_recv, o_keep, lse, q_full, n, slab_width
    )
    grad_slab = jnp.einsum("nrd,nrc->dc", normed_in, grad_proj, preferred_element_type=F32)
    grad_normed_part = jnp.einsum("nrc,dc->nrd", grad_proj, wqkv, preferred_element_type=F32)
    grad_normed, own_slab = reduce_grads(
        n, nb, grad_normed_part.astype(LOW), grad_slab.astype(LOW).reshape(nb, n, shard, slab_width)
    )
    grad_normed = grad_normed.astype(F32)
    own_qkv = (
        own_slab[:, :, : 3 * group_width]
        .reshape(group_count, shard, 3, group_width)
        .transpose(2, 1, 0, 3)
        .reshape(3, shard, width)
    )
    own_grads = jnp.concatenate([own_qkv, own_three], axis=0)

    grad_gain_one = jnp.sum(grad_normed * normed_one, axis=(0, 1))
    input_grad = grad_middle + norm_back(grad_normed * gain_one, normed_one, factor_one)
    own_squares = jnp.sum(own_grads * own_grads)
    scale_slope = LOG_TWO_E / math.sqrt(size) * jax.nn.sigmoid(query_scale)
    scale_part = jnp.sum(scale_part, axis=0)[:size] * scale_slope
    small = jnp.concatenate(
        [grad_gain_one, grad_gain_two, scale_part, stat_terms, own_squares[None]]
    )
    small_rows = (small.shape[0] + 8 * LANES - 1) // (8 * LANES) * 8
    small = jnp.pad(small, (0, small_rows * LANES - small.shape[0])).reshape(small_rows, LANES)
    sums = total_all(n, nb, small).reshape(-1)
    gain_sums = sums[: 2 * width].reshape(2, width)
    scale_grad = sums[2 * width : 2 * width + size]
    stat_sums = sums[2 * width + size : 2 * width + size + 3]
    total_squares = (
        sums[2 * width + size + 3] + jnp.sum(gain_sums * gain_sums) + jnp.sum(scale_grad * scale_grad)
    )
    index = lax.axis_index("batch") * n + lax.axis_index("seq")
    own_gain_grads = lax.dynamic_slice(gain_sums, (0, index * shard), (2, shard))

    grad_norm = jnp.sqrt(total_squares)
    clip_factor = CLIP_NORM / jnp.maximum(grad_norm, CLIP_NORM)
    new_weights, new_first_weights, new_second_weights = adam_update(
        weights, own_grads * clip_factor, first_weights, second_weights, MATRIX_RATE, MATRIX_DECAY
    )
    new_gains, new_first_gains, new_second_gains = adam_update(
        gains, own_gain_grads * clip_factor, first_gains, second_gains, GAIN_RATE, 0.0
    )
    new_scale, new_first_scale, new_second_scale = adam_update(
        query_scale, scale_grad * clip_factor, first_scale, second_scale, GAIN_RATE, 0.0
    )
    rms_stats = jnp.sqrt(stat_sums / float(series_count * rows * width * nb * n))
    return (
        block_out,
        input_grad,
        grad_norm,
        new_weights,
        new_first_weights,
        new_second_weights,
        new_gains,
        new_first_gains,
        new_second_gains,
        new_scale,
        new_first_scale,
        new_second_scale,
        rms_stats,
    )


def solution(mesh):
    return jax.shard_map(
        functools.partial(body, mesh.shape["seq"], mesh.shape["batch"]),
        mesh=mesh,
        in_specs=(
            P("batch", "seq", None),
            P("batch", "seq", None),
            P(None, ("batch", "seq"), None),
            P(None, ("batch", "seq")),
            P(),
            P(None, ("batch", "seq"), None),
            P(None, ("batch", "seq"), None),
            P(None, ("batch", "seq")),
            P(None, ("batch", "seq")),
            P(),
            P(),
            P("batch"),
        ),
        out_specs=(
            P("batch", "seq", None),
            P("batch", "seq", None),
            P(),
            P(None, ("batch", "seq"), None),
            P(None, ("batch", "seq"), None),
            P(None, ("batch", "seq"), None),
            P(None, ("batch", "seq")),
            P(None, ("batch", "seq")),
            P(None, ("batch", "seq")),
            P(),
            P(),
            P(),
            P(),
        ),
        check_vma=False,
    )
```

time: 1630 us -> 537 us (0.33)
  waiting for transfers between devices: 965 us -> 0.06 us
  Pallas kernels: 0 us -> 348 us
  local copies, waits for them, and re-layouts: 238 us -> 99.1 us
  matrix products: 175 us -> 48.2 us
  blocking collectives: 120 us -> 0 us
  other arithmetic: 100 us -> 19.3 us
    reduce_scatter x3 -> x0, waiting for transfers between devices: 697 us -> none  [the longest x1 498 us: body(): lax.psum_scatter(weight_grads, ('batch', 'seq'), scatter_dimension=1, til...]
    pallas_call x0 -> x8, Pallas kernels: none -> 348 us  [the longest x1 99.8 us: reduce_grads(): pl.pallas_call(functools.partial(reduce_kernel, n, nb, chunks), out_shape...]
    all_gather x3 -> x1, waiting for transfers between devices: 267 us -> 0.02 us  [body(): lax.all_gather(low_weights[3:], ('batch', 'seq'), axis=1, tiled=True)]
    dot_general x67 -> x10, matrix products: 170 us -> 46.3 us  [the longest x1 11.4 us: body(): jnp.einsum('nrc,dc->nrd', grad_proj, wqkv, preferred_element_type=F32)]
    dynamic_slice x68 -> x1, local copies, waits for them, and re-layouts: 79.5 us -> 0.6 us  [body(): length = lax.dynamic_slice(lengths, (half,), (1,))]
    dynamic_update_slice x38 -> x0, local copies, waits for them, and re-layouts: 67 us -> none  [the longest x6 48.9 us: body(): lax.map(query_full, (queries, grad_attended, log_totals, all_keys, all_va...]
    concatenate x1 -> x2, local copies, waits for them, and re-layouts: 53.9 us -> 2.74 us  [the longest x1 2.67 us: body(): jnp.concatenate([grad_gain_one, grad_gain_two, scale_part, stat_terms, ow...]
    all_gather x1 -> x0, blocking collectives: 43.2 us -> none  [body(): lax.all_gather(low_gains, ('batch', 'seq'), axis=1, tiled=True)]
  transfers between devices with their start and end apart: 6 -> 2, of which waited for: 6 -> 0; matrix products, arithmetic and copies ran while one was open for 3% -> 11% of each run, Pallas kernels for 0% -> 62%
where the time goes in v1:
time: 537 us; the launch traced here: 532 us
  Pallas kernels  348 us (65%)
  local copies, waits for them, and re-layouts  99.1 us (18%)
  matrix products  48.2 us (9%)
  other arithmetic  19.3 us (4%)
  between operations  17.8 us (3%)
    pallas_call x1, Pallas kernels, reduce_grads(): pl.pallas_call(functools.partial(reduce_kernel, n, nb, chunks), out_shape...  99.8 us
    pallas_call x1, Pallas kernels, gather_tokens(): pl.pallas_call(functools.partial(gather_kernel, n, nb, chunks), out_shape...  99.1 us
    pallas_call x2, Pallas kernels, swap_blocks(): pl.pallas_call(functools.partial(swap_kernel, n), out_shape=jax.ShapeDtyp...  68.3 us
    unnamed x48, local copies, waits for them, and re-layouts  68.1 us
    pallas_call x1, Pallas kernels, attend_back(): pl.pallas_call(functools.partial(attend_back_kernel, heads, size, fold, n...  32 us
    pallas_call x1, Pallas kernels, attend(): pl.pallas_call(functools.partial(attend_kernel, heads, size, fold), grid=...  20.2 us
    pallas_call x1, Pallas kernels, total_all(): pl.pallas_call(functools.partial(total_kernel, n, nb), out_shape=jax.Shap...  15.3 us
    pallas_call x1, Pallas kernels, project(): pl.pallas_call(functools.partial(project_kernel, heads, size), grid=(n,),...  13.1 us
  transfers between devices with their start and end apart: 2, of which 0 were waited for; matrix products, arithmetic and copies ran while one was open for 11% of the time, Pallas kernels for 62%

profile of v1, /device:TPU:0, one launch (start us, length us, event | category | flops | bytes accessed | tf_op | source)
XLA Modules:
  0.0 532.3 jit_solution(17849908490656256463)
XLA Ops:
  11.5 99.1 %gather_tokens.1 = (bf16[8,256,1280]{2,1,0:T(8,128)(2,1)}, bf16[4,8,40,1024]{3,2,1,0:T(8,128)(2,1)}) custom-call(bf16[2,256,1280]{2,1,0:T(8,128)(2,1)} %tok.1, bf16[4,40,1024]{2,1,0:T(8,128)(2,1)} %maximum_maximum_fusion.slab), custom_call_target="tpu_custom_call" | custom-call | tf_op jit(solution)/shard_map/gather_tokens/pallas_call | solution.py:223
  114.4 13.1 %project.1 = (bf16[8,256,1280]{2,1,0:T(8,128)(2,1)}, bf16[12,2048,128]{2,1,0:T(8,128)(2,1)}, f32[4,2048,128]{2,1,0:T(8,128)}) custom-call(bf16[8,256,1280]{2,1,0:T(8,128)(2,1)} %get-tuple-element.25.x_ref, bf16[1280,1024]{1,0:T(8,128)(2,1)S(1)} %bitcast.89, f32[1,1280]{1,0:T(1,128)S(1)} %get-tuple-element.65.gain_ref, f32[1,128]{1,0:T(1,128)S(1)} %pad_bitcast_fusion.1.coef_ref), custom_call_target="tpu_custom_call" | custom-call | tf_op jit(solution)/shard_map/project/pallas_call | solution.py:302
  127.5 20.2 %attend.1 = (bf16[8,128,640]{2,1,0:T(8,128)(2,1)S(1)}, f32[4,2048,128]{2,1,0:T(8,128)S(1)}, f32[4,8,2048]{2,1,0:T(8,128)S(1)}) custom-call(s32[1]{0:T(128)} %dynamic_slice.6.len_ref, bf16[12,2048,128]{2,1,0:T(8,128)(2,1)} %get-tuple-element.27.q_ref.k_ref.v_ref, bf16[12,2048,128]{2,1,0:T(8,128)(2,1)} %get-tuple-element.27.q_ref.k_ref.v_ref, ...), custom_call_target="tpu_custom_call" | custom-call | tf_op jit(solution)/shard_map/attend/pallas_call | solution.py:391
  151.5 36.4 %swap_blocks.2 = bf16[8,128,640]{2,1,0:T(8,128)(2,1)} custom-call(bf16[8,128,640]{2,1,0:T(8,128)(2,1)} %copy-done.3), custom_call_target="tpu_custom_call" | custom-call | tf_op jit(solution)/shard_map/swap_blocks/pallas_call | solution.py:266
  189.6 2.4 copy.77
  192.0 3.5 reshape.98
  195.6 5.1 multiply_reduce_fusion.5
  204.7 2.3 fusion.10
  210.9 4.4 multiply_reduce_fusion
  219.0 55.6 %copy.91 = bf16[3,1280,1280]{2,0,1:T(4,128)(2,1)S(1)} copy(bf16[3,1280,1280]{2,1,0:T(8,128)(2,1)S(1)} %pad_maximum_fusion) | data formatting | bytes 19660800
  274.6 4.8 copy.94
  279.5 5.7 %convolution_convert_fusion.1 = bf16[2,256,1280]{2,1,0:T(8,128)(2,1)} fusion(bf16[3,1280,1280]{2,1,0:T(8,128)(2,1)} %all-gather.2.cloned.1.call-done, f32[2,256,1280]{2,1,0:T(8,128)} %copy-done.7), kind=kOutput, calls=%fused_computation.24 | convolution fusion | flops 1679032320 | bytes 7208960 | tf_op jit(solution)/shard_map/ste,de->std/dot_general | solution.py:863
  285.1 3.5 reshape.115
  288.7 3.2 copy.90
  294.9 31.9 %swap_blocks.3.go_ref = bf16[8,128,640]{2,1,0:T(8,128)(2,1)} custom-call(bf16[8,128,640]{2,1,0:T(8,128)(2,1)} %copy.81.source), custom_call_target="tpu_custom_call" | custom-call | tf_op jit(solution)/shard_map/swap_blocks/pallas_call | solution.py:266
  326.8 32.0 %attend_back.1 = (bf16[8,256,1024]{2,1,0:T(8,128)(2,1)}, f32[8,128]{1,0:T(8,128)}) custom-call(s32[1]{0:T(128)} %dynamic_slice.6.len_ref, f32[1,128]{1,0:T(1,128)} %copy-done.5, bf16[12,2048,128]{2,1,0:T(8,128)(2,1)} %get-tuple-element.27.q_ref.k_ref.v_ref, bf16[12,2048,128]{2,1,0:T(8,128)(2,1)} %get-tuple-element.27.q_ref.k_ref.v_ref, ...), custom_call_target="tpu_custom_call" | custom-call | tf_op jit(solution)/shard_map/attend_back/pallas_call | solution.py:502
  358.8 11.4 %convolution_convert_fusion.gh = bf16[8,256,1280]{2,1,0:T(8,128)(2,1)} fusion(bf16[8,256,1024]{2,1,0:T(8,128)(2,1)} %get-tuple-element.32, bf16[1280,1024,1]{1,0,2:T(8,128)(2,1)S(1)} %bitcast.90), kind=kOutput, calls=%fused_computation.10 | convolution fusion | flops 5371330560 | bytes 12058624 | tf_op jit(solution)/shard_map/nrc,dc->nrd/dot_general | solution.py:883
  370.2 9.6 %bitcast_convert_fusion = bf16[1280,1024]{1,0:T(8,128)(2,1)} fusion(bf16[8,256,1280]{2,1,0:T(8,128)(2,1)} %get-tuple-element.33, bf16[8,256,1024]{2,1,0:T(8,128)(2,1)S(1)} %copy-done.20), kind=kOutput, calls=%fused_computation.11 | convolution fusion | flops 5370019840 | bytes 12058624 | tf_op jit(solution)/shard_map/nrd,nrc->dc/dot_general | solution.py:882
  379.8 99.8 %reduce_grads.1 = (bf16[2,256,1280]{2,1,0:T(8,128)(2,1)}, f32[4,40,1024]{2,1,0:T(8,128)}) custom-call(bf16[8,256,1280]{2,1,0:T(8,128)(2,1)} %convolution_convert_fusion.gh, bf16[4,8,40,1024]{3,2,1,0:T(8,128)(2,1)} %bitcast.97), custom_call_target="tpu_custom_call" | custom-call | tf_op jit(solution)/shard_map/reduce_grads/pallas_call | solution.py:687
  479.6 2.4 reshape.102
  482.0 2.5 copy.83
  492.3 2.7 concatenate.15
  495.6 15.3 %total_all.1 = f32[24,128]{1,0:T(8,128)} custom-call(f32[24,128]{1,0:T(8,128)} %pad_bitcast_fusion.value), custom_call_target="tpu_custom_call" | custom-call | tf_op jit(solution)/shard_map/total_all/pallas_call | solution.py:759
  519.3 4.2 multiply_subtract_fusion
  (96 shorter events, 43.4 us)
Async XLA Ops:
  7.2 2.3 copy-start.13
  7.2 188.4 %all-gather.2.cloned.1.call-start = ((), (), s32[]{:S(2)}) async-start(), calls=%async_computation.1 | async-start | bytes 10137600 | tf_op jit(solution)/shard_map/all_gather | solution.py:815
  9.4 480.8 %reduce-scatter.4.cloned.1.call-start = ((), (), s32[]{:S(2)}) async-start(), calls=%async_computation.2 | async-start | bytes 10137600
  10.2 101.7 %copy-start.21 = (s32[2]{0:T(128)S(1)}, s32[2]{0:T(128)}, u32[]{:S(2)}) copy-start(s32[2]{0:T(128)} %param.23) | copy-start | bytes 28
  10.3 102.3 %copy-start.16 = (f32[80]{0:T(128)S(1)}, f32[80]{0:T(128)}, u32[]{:S(2)}) copy-start(f32[80]{0:T(128)} %param.16) | copy-start | bytes 964
  112.6 14.9 %copy-start.5 = (f32[1,128]{1,0:T(1,128)}, f32[1,128]{1,0:T(1,128)S(1)}, u32[]{:S(2)}) copy-start(f32[1,128]{1,0:T(1,128)S(1)} %pad_bitcast_fusion.1.coef_ref) | copy-start | bytes 1540
  112.7 1.7 copy-start.1
  147.7 2.0 copy-start
  149.7 1.1 copy-start.3
  150.8 0.7 copy-start.4
  189.6 6.0 %copy-start.6 = (bf16[2,256,1280]{2,1,0:T(8,128)(2,1)S(1)}, bf16[2,256,1280]{2,1,0:T(8,128)(2,1)}, u32[]{:S(2)}) copy-start(bf16[2,256,1280]{2,1,0:T(8,128)(2,1)} %tok.1) | copy-start | bytes 3932164
  195.6 5.2 copy-start.19
  200.8 2.0 copy-start.11
  215.9 1.9 copy-start.7
  326.8 32.0 %copy-start.2 = (bf16[4,8,40,1024]{3,2,1,0:T(8,128)(2,1)S(1)}, bf16[4,8,40,1024]{3,2,1,0:T(8,128)(2,1)}, u32[]{:S(2)}) copy-start(bf16[4,8,40,1024]{3,2,1,0:T(8,128)(2,1)} %get-tuple-element.26) | copy-start | bytes 7864324
  358.8 11.4 %copy-start.20 = (bf16[8,256,1024]{2,1,0:T(8,128)(2,1)S(1)}, bf16[8,256,1024]{2,1,0:T(8,128)(2,1)}, u32[]{:S(2)}) copy-start(bf16[8,256,1024]{2,1,0:T(8,128)(2,1)} %get-tuple-element.32) | copy-start | bytes 12582916
  479.6 6.6 %copy-start.12 = (f32[8,128]{1,0:T(8,128)S(1)}, f32[8,128]{1,0:T(8,128)}, u32[]{:S(2)}) copy-start(f32[8,128]{1,0:T(8,128)} %get-tuple-element.35) | copy-start | bytes 12292
  479.6 6.6 %copy-start.9 = (bf16[2,256,1280]{2,1,0:T(8,128)(2,1)S(1)}, bf16[2,256,1280]{2,1,0:T(8,128)(2,1)}, u32[]{:S(2)}) copy-start(bf16[2,256,1280]{2,1,0:T(8,128)(2,1)} %get-tuple-element.34) | copy-start | bytes 3932164
  486.2 1.7 copy-start.8
  490.1 27.9 %copy-start.17 = (f32[80]{0:T(128)S(1)}, f32[80]{0:T(128)}, u32[]{:S(2)}) copy-start(f32[80]{0:T(128)} %param.21) | copy-start | bytes 964
  490.1 27.9 %copy-start.18 = (f32[80]{0:T(128)S(1)}, f32[80]{0:T(128)}, u32[]{:S(2)}) copy-start(f32[80]{0:T(128)} %param.22) | copy-start | bytes 964
  490.1 29.2 %copy-start.10 = (f32[6,40,1280]{2,1,0:T(8,128)S(1)}, f32[6,40,1280]{2,1,0:T(8,128)}, u32[]{:S(2)}) copy-start(f32[6,40,1280]{2,1,0:T(8,128)} %param.14) | copy-start | bytes 3686404
  519.3 4.2 copy-start.14
  519.3 4.2 copy-start.15
Sparse Core Ops, SparseCore 0:
  11.5 109.6 all-gather.1
  279.6 169.9 reduce-scatter.3

commit v2 on v1

--- a/solution.py
+++ b/solution.py
@@ -101,9 +101,72 @@
     return (1 - half) * (half_chips + step) + half * (half_chips - 1 - step)
 
 
+def batch_neighbours(batch):
+    across = lax.rem(batch, 2)
+    first = batch + 1 - 2 * across
+    second = lax.rem(batch + 2, 4)
+    return (first, second), lax.rem(first + 2, 4)
+
+
+class Spread:
+    def __init__(self, nb, ref, send, recv):
+        self.nb, self.ref, self.send, self.recv = nb, ref, send, recv
+        self.batch = lax.axis_index("batch")
+        self.copies = []
+
+    def copy(self, owner, slot, j, lane, target):
+        block = self.ref.at[owner, slot]
+        return push(block, block, self.send.at[j, lane], self.recv.at[j, lane], batch=target)
+
+    def route(self, lane):
+        sides, across = batch_neighbours(self.batch)
+        return sides[lane % 2], sides[1 - lane % 2], across
+
+    def begin(self, slot, lane):
+        if self.nb == 4:
+            first, second, _ = self.route(lane)
+            new = [self.copy(self.batch, slot, 0, lane, first), self.copy(self.batch, slot, 1, lane, second)]
+        else:
+            new = [
+                self.copy(self.batch, slot, j - 1, lane, lax.rem(self.batch + j, self.nb))
+                for j in range(1, self.nb)
+            ]
+        for copy in new:
+            copy.start()
+        self.copies += new
+
+    def relay(self, slot, lane):
+        if self.nb == 4:
+            first, second, _ = self.route(lane)
+            self.copy(first, slot, 0, lane, first).wait_recv()
+            copy = self.copy(first, slot, 2, lane, second)
+            copy.start()
+            self.copies.append(copy)
+            return [first]
+        return []
+
+    def finish(self, slot, lane):
+        if self.nb == 4:
+            _, second, across = self.route(lane)
+            self.copy(second, slot, 1, lane, second).wait_recv()
+            self.copy(across, slot, 2, lane, second).wait_recv()
+            return [second, across]
+        owners = []
+        for j in range(1, self.nb):
+            owner = lax.rem(self.batch + self.nb - j, self.nb)
+            self.copy(owner, slot, j - 1, lane, owner).wait_recv()
+            owners.append(owner)
+        return owners
+
+    def drain(self):
+        for copy in self.copies:
+            copy.wait_send()
+
+
 def gather_kernel(
-    n, nb, chunks, tok, slab, xg, wout, far_sem, own_sem, pass_sem, sib_sem, same_recv, sib_recv,
-    z_send, z_recv, b_send, b_recv, local_sem,
+    n, nb, chunks, tok, slab, own_w, xg, wout, w_all, far_sem, own_sem, pass_sem, sib_sem, same_recv,
+    sib_recv, z_send, z_recv, b_send, b_recv, wz_send, wz_recv, wb_send, wb_recv, ws_send, ws_recv,
+    local_sem,
 ):
     chips, half_chips = n // 2, n // 4
     me, core, chip, half, base, gate_mine, gate_other = place(n)
@@ -113,6 +176,7 @@
     sibling = 2 * chip + 1 - core
     greet(n, nb)
 
+    sends = []
     z_copies = []
     for k in range(1, n):
         target = lax.rem(me + k, n)
@@ -122,6 +186,12 @@
         )
         copy.start()
         z_copies.append(copy)
+    w_copies = []
+    for k in range(1, chips):
+        target = 2 * lax.rem(chip + k, chips) + core
+        copy = push(own_w, w_all.at[batch, me], wz_send.at[k], wz_recv.at[k], seq=target)
+        copy.start()
+        w_copies.append(copy)
 
     def part(ref, lead, c):
         return ref.at[lead, pl.ds(c * rows, rows)]
@@ -129,7 +199,6 @@
     def tok_copy(source, slot, c, send_sem, recv_sem, target):
         return push(source, part(xg, slot, c), send_sem, recv_sem.at[slot, c], seq=target)
 
-    sends = []
     for c in range(chunks):
         copy = tok_copy(
             part(tok, 1 - half, c), me, c, far_sem.at[c], same_recv, 2 * gate_other + core
@@ -152,29 +221,30 @@
         slab.at[lax.rem(me, group_count)], wout.at[batch, me], local_sem.at[1]
     )
     slab_copy.start()
+    w_copy = pltpu.make_async_copy(own_w, w_all.at[batch, me], local_sem.at[2])
+    w_copy.start()
     slab_copy.wait()
-
-    b_copies = []
-
-    def spread(source, index):
-        for j in range(1, nb):
-            copy = push(
-                wout.at[batch, source], wout.at[batch, source], b_send.at[j, index],
-                b_recv.at[j, index], batch=lax.rem(batch + j, nb),
-            )
-            copy.start()
-            b_copies.append(copy)
-
-    spread(me, 0)
-    for k in range(1, n):
-        z_copies[k - 1].wait_recv()
-        spread(lax.rem(me + n - k, n), k)
-
-    for c in range(chunks):
+    w_copy.wait()
+
+    slices = Spread(nb, wout, b_send, b_recv)
+    whole = Spread(nb, w_all, wb_send, wb_recv)
+
+    def line_slot(k):
+        return lax.rem(me + n - k, n)
+
+    def chip_slot(k):
+        return 2 * lax.rem(chip + chips - k, chips) + core
+
+    def to_sibling(owner, lane, slot, j):
+        block = w_all.at[owner, slot]
+        copy = push(block, block, ws_send.at[j, lane], ws_recv.at[owner, slot], seq=sibling)
+        copy.start()
+        sends.append(copy)
+
+    def pass_tokens(c):
         for k in range(1, half_chips):
             slot = 2 * (base + lax.rem(chip - base + half_chips - k, half_chips)) + core
-            arrived = tok_copy(part(xg, slot, c), slot, c, sib_sem.at[k, c], same_recv, sibling)
-            arrived.wait_recv()
+            tok_copy(part(xg, slot, c), slot, c, sib_sem.at[k, c], same_recv, sibling).wait_recv()
             copy = tok_copy(part(xg, slot, c), slot, c, sib_sem.at[k, c], sib_recv, sibling)
             copy.start()
             sends.append(copy)
@@ -196,14 +266,46 @@
             copy.start()
             sends.append(copy)
 
+    slices.begin(me, 0)
+    whole.begin(me, 0)
+    to_sibling(batch, 0, me, 0)
+    for k in range(1, n):
+        z_copies[k - 1].wait_recv()
+        slices.begin(line_slot(k), k)
+    pass_tokens(0)
+    for k in range(1, chips):
+        w_copies[k - 1].wait_recv()
+        whole.begin(chip_slot(k), k)
+        to_sibling(batch, k, chip_slot(k), 0)
+    pass_tokens(1)
+    for k in range(n):
+        slices.relay(line_slot(k), k)
+    pass_tokens(2)
+    for k in range(chips):
+        for j, owner in enumerate(whole.relay(chip_slot(k), k)):
+            to_sibling(owner, k, chip_slot(k), 1 + j)
+    pass_tokens(3)
+    for k in range(n):
+        slices.finish(line_slot(k), k)
+    for k in range(chips):
+        owners = whole.finish(chip_slot(k), k)
+        for j, owner in enumerate(owners):
+            to_sibling(owner, k, chip_slot(k), nb - len(owners) + j)
+
     for c in range(chunks):
         for q in range(chips):
             slot = 2 * q + 1 - core
             tok_copy(part(xg, slot, c), slot, c, sib_sem.at[0, c], sib_recv, sibling).wait_recv()
+    for owner in range(nb):
+        for q in range(chips):
+            block = w_all.at[owner, 2 * q + 1 - core]
+            push(
+                block, block, ws_send.at[0, 0], ws_recv.at[owner, 2 * q + 1 - core], seq=sibling
+            ).wait_recv()
     own_copy.wait()
-    for copy in b_copies:
-        copy.wait_recv()
-    for copy in sends + b_copies + z_copies:
+    slices.drain()
+    whole.drain()
+    for copy in sends + z_copies + w_copies:
         copy.wait_send()
 
     @pl.when(chip == gate_mine)
@@ -216,7 +318,7 @@
                     ).wait_send()
 
 
-def gather_tokens(n, nb, tokens, slab):
+def gather_tokens(n, nb, tokens, slab, own_w):
     chunks = 4
     chips, half_chips = n // 2, n // 4
     dma = pltpu.SemaphoreType.DMA
@@ -225,9 +327,10 @@
         out_shape=(
             jax.ShapeDtypeStruct((n,) + tokens.shape[1:], tokens.dtype),
             jax.ShapeDtypeStruct((nb, n) + slab.shape[1:], slab.dtype),
+            jax.ShapeDtypeStruct((nb, n) + own_w.shape, own_w.dtype),
         ),
-        in_specs=[pl.BlockSpec(memory_space=pl.ANY)] * 2,
-        out_specs=[pl.BlockSpec(memory_space=pl.ANY)] * 2,
+        in_specs=[pl.BlockSpec(memory_space=pl.ANY)] * 3,
+        out_specs=[pl.BlockSpec(memory_space=pl.ANY)] * 3,
         scratch_shapes=[
             dma((chunks,)),
             dma((half_chips, chunks)),
@@ -239,11 +342,17 @@
             dma((n,)),
             dma((nb, n)),
             dma((nb, n)),
-            dma((2,)),
+            dma((chips,)),
+            dma((chips,)),
+            dma((nb, chips)),
+            dma((nb, chips)),
+            dma((nb, chips)),
+            dma((nb, n)),
+            dma((3,)),
         ],
         compiler_params=pltpu.CompilerParams(collective_id=1, has_side_effects=True),
         name="gather_tokens",
-    )(tokens, slab)
+    )(tokens, slab, own_w)
 
 
 def swap_kernel(n, source, target, send_sem, recv_sem, local_sem):
@@ -535,10 +644,189 @@
     )(length, coef, qkv, qkv, qkv, go, keep, lse, q_full)
 
 
+def fold_rows(values):
+    rows, width = values.shape
+    return jnp.sum(values.reshape(rows // 8, 8, width), axis=0)
+
+
+def layer_kernel(
+    n, nb, fold, tok, cot, o_in, w_in, gain_ref, y_out, gy_out, go_out, small_out, half_out,
+    w, o_s, hidden_s, act_s, gu_s, ga_s, go_s, gw_s, sib_in, w_sem, send_sem, recv_sem, local_sem,
+    sib_send, sib_recv,
+):
+    group_count = n // 2
+    me, core, chip, half, base, gate_mine, gate_other = place(n)
+    sibling = 2 * chip + 1 - core
+    _, rows, width = tok.shape
+    group_width = width // group_count
+    piece = rows // fold
+    barrier = pltpu.get_barrier_semaphore()
+    for k in range(1, n):
+        pl.semaphore_signal(
+            barrier, inc=1, device_id={"seq": lax.rem(me + k, n)}, device_id_type=MESH
+        )
+    loads = [pltpu.make_async_copy(w_in.at[m], w.at[m], w_sem.at[m]) for m in range(3)]
+    for load in loads:
+        load.start()
+    small_out[...] = jnp.zeros_like(small_out)
+    gain = gain_ref[...]
+
+    def go_push(target):
+        return push(
+            go_s.at[target], go_out.at[me], send_sem.at[target], recv_sem.at[me], seq=target
+        )
+
+    own_go = pltpu.make_async_copy(go_s.at[me], go_out.at[me], local_sem)
+
+    for t in range(2):
+        parts = [
+            jnp.concatenate(
+                [
+                    o_in[t * group_count + g, :, f * group_width : (f + 1) * group_width]
+                    for g in range(group_count)
+                ],
+                axis=1,
+            )
+            for f in range(fold)
+        ]
+        o = jnp.concatenate(parts, axis=0)
+        o_s[t] = o
+        if t == 0:
+            loads[0].wait()
+        a = dot(o, w[0])
+        small_out[1] += fold_rows(a * a)
+        y1 = tok[t].astype(F32) + a
+        factor = rms_factor(y1)
+        normed = y1 * factor
+        hidden = (normed * gain).astype(LOW)
+        hidden_s[t] = hidden
+        if t == 0:
+            loads[1].wait()
+        u = dot(hidden, w[1])
+        logistic = 1.0 / (1.0 + jnp.exp(-u))
+        act = (u * logistic).astype(LOW)
+        act_s[t] = act
+        if t == 0:
+            loads[2].wait()
+        f = dot(act, w[2])
+        small_out[2] += fold_rows(f * f)
+        y = y1 + f
+        small_out[3] += fold_rows(y * y)
+        y_out[t] = y.astype(LOW)
+        gz = dot(cot[t], w[2], 1, 1)
+        gu = (gz * (logistic * (1.0 + u * (1.0 - logistic)))).astype(LOW)
+        gu_s[t] = gu
+        gh = dot(gu, w[1], 1, 1)
+        small_out[0] += fold_rows(gh * normed)
+        gy = cot[t].astype(F32) + norm_back(gh * gain, normed, factor)
+        gy_out[t] = gy
+        ga = gy.astype(LOW)
+        ga_s[t] = ga
+        go = dot(ga, w[0], 1, 1).astype(LOW)
+        for g in range(group_count):
+            block = go[:, g * group_width : (g + 1) * group_width]
+            go_s[t * group_count + g] = jnp.concatenate(
+                [block[f * piece : (f + 1) * piece] for f in range(fold)], axis=1
+            )
+        if t == 0:
+            pl.semaphore_wait(barrier, n - 1)
+        for g in range(group_count):
+            target = t * group_count + g
+
+            @pl.when(target != me)
+            def _():
+                go_push(target).start()
+
+            @pl.when(target == me)
+            def _():
+                own_go.start()
+
+    tile = 256
+    half_rows = width // nb // 2
+    sib_copies = []
+    pairs = ((act_s, cot, 2), (hidden_s, gu_s, 1), (o_s, ga_s, 0))
+    for left, right, m in pairs:
+
+        @pl.loop(0, width // tile)
+        def _(k):
+            cols = pl.ds(pl.multiple_of(k * tile, tile), tile)
+            total = dot(left[0, :, cols], right[0], 0, 0) + dot(left[1, :, cols], right[1], 0, 0)
+            gw_s[m, cols] = total.astype(LOW)
+
+        for b in range(nb):
+            start = pl.multiple_of((2 * b + 1 - core) * half_rows, 16)
+            copy = push(
+                gw_s.at[m, pl.ds(start, half_rows)], sib_in.at[b, m], sib_send.at[b, m],
+                sib_recv.at[b, m], seq=sibling,
+            )
+            copy.start()
+            sib_copies.append(copy)
+    index = 0
+    for _, _, m in pairs:
+        for b in range(nb):
+            sib_copies[index].wait_recv()
+            index += 1
+            start = pl.multiple_of((2 * b + core) * half_rows, 16)
+            half_out[b, m] = (
+                gw_s[m, pl.ds(start, half_rows)].astype(F32) + sib_in[b, m].astype(F32)
+            ).astype(LOW)
+    for k in range(1, n):
+        source = lax.rem(me + k, n)
+        push(
+            go_s.at[source], go_out.at[source], send_sem.at[source], recv_sem.at[source], seq=source
+        ).wait()
+    own_go.wait()
+    for copy in sib_copies:
+        copy.wait_send()
+
+
+def layer(n, nb, fold, tokens, cotangent, o_recv, w_all, gain):
+    _, rows, width = tokens.shape
+    half_rows = width // nb // 2
+    dma = pltpu.SemaphoreType.DMA
+    vmem = pl.BlockSpec(memory_space=pltpu.VMEM)
+    anywhere = pl.BlockSpec(memory_space=pl.ANY)
+    kept = pltpu.VMEM((2, rows, width), LOW)
+    return pl.pallas_call(
+        functools.partial(layer_kernel, n, nb, fold),
+        out_shape=(
+            jax.ShapeDtypeStruct((2, rows, width), LOW),
+            jax.ShapeDtypeStruct((2, rows, width), F32),
+            jax.ShapeDtypeStruct(o_recv.shape, LOW),
+            jax.ShapeDtypeStruct((4, 8, width), F32),
+            jax.ShapeDtypeStruct((nb, 3, half_rows, width), LOW),
+        ),
+        in_specs=[vmem, vmem, vmem, anywhere, vmem],
+        out_specs=[vmem, vmem, anywhere, vmem, vmem],
+        scratch_shapes=[
+            pltpu.VMEM((3, width, width), LOW),
+            kept,
+            kept,
+            kept,
+            kept,
+            kept,
+            pltpu.VMEM(o_recv.shape, LOW),
+            pltpu.VMEM((3, width, width), LOW),
+            pltpu.VMEM((nb, 3, half_rows, width), LOW),
+            dma((3,)),
+            dma((n,)),
+            dma((n,)),
+            dma,
+            dma((nb, 3)),
+            dma((nb, 3)),
+        ],
+        compiler_params=pltpu.CompilerParams(
+            collective_id=3, has_side_effects=True, vmem_limit_bytes=63 * MIB
+        ),
+        name="layer",
+    )(tokens, cotangent, o_recv, w_all, gain)
+
+
 def reduce_kernel(
-    n, nb, chunks, gh, gw, out, own_gw, from_sib, total, gate_in, peer_in, batch_in, line_out, line_in,
-    sib_send, sib_recv, gate_send, gate_recv, peer_send, peer_recv, far_send, far_recv,
-    b_send, b_recv, z_send, z_recv,
+    n, nb, chunks, gh, gw, w_half, out, own_gw, own_w, from_sib, total, gate_in, peer_in, batch_in,
+    line_out, line_in, cross_in, cross_out, turn_in, w_line, w_in, sib_send, sib_recv, gate_send,
+    gate_recv, peer_send, peer_recv, far_send, far_recv, b_send, b_recv, z_send, z_recv, c_send,
+    c_recv, t_send, t_recv, w_send, w_recv,
 ):
     chips, half_chips = n // 2, n // 4
     me, core, chip, half, base, gate_mine, gate_other = place(n)
@@ -547,6 +835,32 @@
     rows = gh.shape[1] // chunks
     sibling = 2 * chip + 1 - core
     greet(n, nb)
+
+    split = 2 if nb == 4 else 1
+    w_rows = w_half.shape[2] // split
+    sides, across = batch_neighbours(batch)
+
+    def w_part(b, h):
+        return w_half.at[b, :, pl.ds(h * w_rows, w_rows)]
+
+    w_copies = []
+    if nb == 4:
+        for h in range(2):
+            for j, owner in enumerate((across, sides[h])):
+                copy = push(
+                    w_part(owner, h), cross_in.at[h, j], c_send.at[h, j], c_recv.at[h, j],
+                    batch=sides[h],
+                )
+                copy.start()
+                w_copies.append(copy)
+    else:
+        for k in range(1, nb):
+            target = lax.rem(batch + k, nb)
+            copy = push(
+                w_half.at[target], cross_in.at[0, k], c_send.at[0, k], c_recv.at[0, k], batch=target
+            )
+            copy.start()
+            w_copies.append(copy)
 
     b_copies = []
     for k in range(1, nb):
@@ -624,6 +938,20 @@
 
     add_sibling(chips - 1)
 
+    t_copies = []
+    if nb == 4:
+        for h in range(2):
+            w_copies[2 * h].wait_recv()
+            span = pl.ds(h * w_rows, w_rows)
+            cross_out[h] = (
+                w_half[sides[1 - h], :, span].astype(F32) + cross_in[h, 0].astype(F32)
+            ).astype(LOW)
+            copy = push(
+                cross_out.at[h], turn_in.at[h], t_send.at[h], t_recv.at[h], batch=sides[1 - h]
+            )
+            copy.start()
+            t_copies.append(copy)
+
     for copy in b_copies:
         copy.wait_recv()
 
@@ -641,6 +969,43 @@
         copy.start()
         z_copies.append(copy)
     line_in[me] = line_out[me]
+
+    shard = own_w.shape[1]
+    parts = []
+    if nb == 4:
+        for h in range(2):
+            w_copies[2 * h + 1].wait_recv()
+            t_copies[h].wait_recv()
+            span = pl.ds(h * w_rows, w_rows)
+            parts.append(
+                w_half[batch, :, span].astype(F32)
+                + cross_in[h, 1].astype(F32)
+                + turn_in[h].astype(F32)
+            )
+    else:
+        value = w_half[batch].astype(F32)
+        for k in range(1, nb):
+            w_copies[k - 1].wait_recv()
+            value = value + cross_in[0, k].astype(F32)
+        parts.append(value)
+    summed = jnp.concatenate(parts, axis=1)
+    for i in range(group_count):
+        w_line[i] = summed[:, i * shard : (i + 1) * shard].astype(LOW)
+
+    def w_push(i):
+        target = core * group_count + i
+        return push(w_line.at[i], w_in.at[chip], w_send.at[i], w_recv.at[chip], seq=target)
+
+    for i in range(group_count):
+        mine = core * group_count + i == me
+
+        @pl.when(mine)
+        def _():
+            w_in[chip] = w_line[i]
+
+        @pl.when(jnp.logical_not(mine))
+        def _():
+            w_push(i).start()
 
     value = total[chip].astype(F32)
     for k in range(1, half_chips):
@@ -658,7 +1023,25 @@
     for g in range(group_count):
         own_gw[g] = line_in[g].astype(F32) + line_in[g + group_count].astype(F32)
 
-    for copy in b_copies + sib_copies + z_copies:
+    for q in range(chips):
+
+        @pl.when(2 * q + half != me)
+        def _():
+            push(
+                w_line.at[0], w_in.at[q], w_send.at[0], w_recv.at[q], seq=sibling
+            ).wait_recv()
+
+    value = w_in[0].astype(F32)
+    for q in range(1, chips):
+        value = value + w_in[q].astype(F32)
+    own_w[...] = value
+    for i in range(group_count):
+
+        @pl.when(core * group_count + i != me)
+        def _():
+            w_push(i).wait_send()
+
+    for copy in b_copies + sib_copies + z_copies + w_copies + t_copies:
         copy.wait_send()
     for k in range(1, half_chips):
         push(
@@ -678,20 +1061,24 @@
                 gate_copy(1, k, c).wait_send()
 
 
-def reduce_grads(n, nb, gh, gw):
+def reduce_grads(n, nb, gh, gw, w_half, shard):
     chunks = 4
     chips, half_chips = n // 2, n // 4
     _, rows, width = gh.shape
     slab = gw.shape[2:]
+    half_rows = w_half.shape[2]
+    split = 2 if nb == 4 else 1
+    steps = 2 if nb == 4 else nb
     dma = pltpu.SemaphoreType.DMA
     return pl.pallas_call(
         functools.partial(reduce_kernel, n, nb, chunks),
         out_shape=(
             jax.ShapeDtypeStruct((2, rows, width), LOW),
             jax.ShapeDtypeStruct((n // 2,) + slab, F32),
+            jax.ShapeDtypeStruct((3, shard, width), F32),
         ),
-        in_specs=[pl.BlockSpec(memory_space=pltpu.VMEM)] * 2,
-        out_specs=[pl.BlockSpec(memory_space=pltpu.VMEM)] * 2,
+        in_specs=[pl.BlockSpec(memory_space=pltpu.VMEM)] * 3,
+        out_specs=[pl.BlockSpec(memory_space=pltpu.VMEM)] * 3,
         scratch_shapes=[
             pltpu.VMEM((chips, rows, width), LOW),
             pltpu.VMEM((chips, rows, width), LOW),
@@ -700,6 +1087,11 @@
             pltpu.VMEM((nb, n) + slab, LOW),
             pltpu.VMEM((n,) + slab, LOW),
             pltpu.VMEM((n,) + slab, LOW),
+            pltpu.VMEM((split, steps, 3, half_rows // split, width), LOW),
+            pltpu.VMEM((split, 3, half_rows // split, width), LOW),
+            pltpu.VMEM((split, 3, half_rows // split, width), LOW),
+            pltpu.VMEM((n // 2, 3, shard, width), LOW),
+            pltpu.VMEM((chips, 3, shard, width), LOW),
             dma((chips,)),
             dma((chips,)),
             dma((half_chips, chunks)),
@@ -712,12 +1104,18 @@
             dma((nb,)),
             dma((n,)),
             dma((n,)),
+            dma((split, steps)),
+            dma((split, steps)),
+            dma((split,)),
+            dma((split,)),
+            dma((n // 2,)),
+            dma((chips,)),
         ],
         compiler_params=pltpu.CompilerParams(
-            collective_id=4, has_side_effects=True, vmem_limit_bytes=60 * MIB
+            collective_id=4, has_side_effects=True, vmem_limit_bytes=63 * MIB
         ),
         name="reduce_grads",
-    )(gh, gw)
+    )(gh, gw, w_half)
 
 
 def total_kernel(n, nb, value, out, mine, line_in, batch_in, z_send, z_recv, b_send, b_recv):
@@ -812,77 +1210,36 @@
     low_gains = jnp.broadcast_to(gains.astype(LOW).T[None], (group_count, shard, 2))
     spare = jnp.zeros((group_count, shard, slab_width - 3 * group_width - 2), LOW)
     slab = jnp.concatenate([slab, low_gains, spare], axis=2)
-    full_weights = lax.all_gather(low_weights[3:], ("batch", "seq"), axis=1, tiled=True)
-
-    xg, wout = gather_tokens(n, nb, tokens, slab)
+
+    xg, wout, w_all = gather_tokens(n, nb, tokens, slab, low_weights[3:])
+    w_all = w_all.transpose(2, 0, 1, 3, 4).reshape(3, width, width)
     wqkv = wout.reshape(nb * n * shard, slab_width)
     gain_rows = wqkv[:, 3 * group_width : 3 * group_width + 2].astype(F32).T
-    gain_one, gain_two = gain_rows[0:1], gain_rows[1]
+    gain_one, gain_two = gain_rows[0:1], gain_rows[1:2]
 
     coef = LOG_TWO_E / math.sqrt(size) * jax.nn.softplus(query_scale)
     coef_row = jnp.concatenate([coef, jnp.zeros((LANES - size,), F32)])[None]
     normed_in, qkv, q_full = project(heads, size, xg, wqkv, gain_one, coef_row)
     o_send, o_keep, lse = attend(heads, size, fold, length, qkv, n)
     o_recv = swap_blocks(n, o_send, 2)
-    attended_low = (
-        o_recv.reshape(2, group_count, rows // fold, fold, group_width)
-        .transpose(0, 3, 2, 1, 4)
-        .reshape(2, rows, width)
-    )
-
+    block_out, grad_middle, go_recv, layer_sums, w_half = layer(
+        n, nb, fold, tokens, cotangent, o_recv, w_all, gain_two
+    )
+    layer_sums = jnp.sum(layer_sums, axis=1)
+    grad_gain_two = layer_sums[0]
+    stat_terms = jnp.sum(layer_sums[1:], axis=1)
     inputs = tokens.astype(F32)
     factor_one = rms_factor(inputs)
     normed_one = inputs * factor_one
-    branch_one = jnp.einsum("std,de->ste", attended_low, full_weights[0], preferred_element_type=F32)
-    middle = inputs + branch_one
-    factor_two = rms_factor(middle)
-    normed_two = middle * factor_two
-    hidden_in = (normed_two * gain_two).astype(LOW)
-    pre_act = jnp.einsum("std,de->ste", hidden_in, full_weights[1], preferred_element_type=F32)
-    activated = jax.nn.silu(pre_act).astype(LOW)
-    branch_two = jnp.einsum("std,de->ste", activated, full_weights[2], preferred_element_type=F32)
-    final_sum = middle + branch_two
-    block_out = final_sum.astype(LOW)
-    stat_terms = jnp.stack(
-        [
-            jnp.sum(branch_one * branch_one),
-            jnp.sum(branch_two * branch_two),
-            jnp.sum(final_sum * final_sum),
-        ]
-    )
-    grad_out = cotangent.astype(F32)
-    grad_down = jnp.einsum("std,ste->de", activated, cotangent, preferred_element_type=F32)
-    grad_act = jnp.einsum("ste,de->std", cotangent, full_weights[2], preferred_element_type=F32)
-    grad_pre = (grad_act * silu_slope(pre_act)).astype(LOW)
-    grad_up = jnp.einsum("std,ste->de", hidden_in, grad_pre, preferred_element_type=F32)
-    grad_hidden = jnp.einsum("ste,de->std", grad_pre, full_weights[1], preferred_element_type=F32)
-    grad_gain_two = jnp.sum(grad_hidden * normed_two, axis=(0, 1))
-    grad_middle = grad_out + norm_back(grad_hidden * gain_two, normed_two, factor_two)
-    grad_branch = grad_middle.astype(LOW)
-    grad_out_proj = jnp.einsum("std,ste->de", attended_low, grad_branch, preferred_element_type=F32)
-    grad_attended = jnp.einsum(
-        "ste,de->std", grad_branch, full_weights[0], preferred_element_type=F32
-    ).astype(LOW)
-    go_send = (
-        grad_attended.reshape(2, fold, rows // fold, group_count, group_width)
-        .transpose(0, 3, 2, 1, 4)
-        .reshape(n, rows // fold, fold * group_width)
-    )
-    go_recv = swap_blocks(n, go_send, 3)
-    own_three = lax.psum_scatter(
-        jnp.stack([grad_out_proj, grad_up, grad_down]).astype(LOW),
-        ("batch", "seq"),
-        scatter_dimension=1,
-        tiled=True,
-    ).astype(F32)
 
     grad_proj, scale_part = attend_back(
         heads, size, fold, length, coef_row, qkv, go_recv, o_keep, lse, q_full, n, slab_width
     )
     grad_slab = jnp.einsum("nrd,nrc->dc", normed_in, grad_proj, preferred_element_type=F32)
     grad_normed_part = jnp.einsum("nrc,dc->nrd", grad_proj, wqkv, preferred_element_type=F32)
-    grad_normed, own_slab = reduce_grads(
-        n, nb, grad_normed_part.astype(LOW), grad_slab.astype(LOW).reshape(nb, n, shard, slab_width)
+    grad_normed, own_slab, own_three = reduce_grads(
+        n, nb, grad_normed_part.astype(LOW),
+        grad_slab.astype(LOW).reshape(nb, n, shard, slab_width), w_half, shard,
     )
     grad_normed = grad_normed.astype(F32)
     own_qkv = (

time: 537 us -> 488 us (0.909)
  local copies, waits for them, and re-layouts: 99.1 us -> 25 us
  Pallas kernels: 348 us -> 417 us
  matrix products: 48.2 us -> 17.4 us
  between operations: 17.8 us -> 4.55 us
    unnamed x48 -> x45, local copies, waits for them, and re-layouts: 68.1 us -> 7.54 us
    pallas_call x2 -> x1, Pallas kernels: 68.3 us -> 22.6 us  [swap_blocks(): pl.pallas_call(functools.partial(swap_kernel, n), out_shape=jax.ShapeDtyp...]
    pallas_call x0 -> x1, Pallas kernels: none -> 42.5 us  [layer(): pl.pallas_call(functools.partial(layer_kernel, n, nb, fold), out_shape=(j...]
    dot_general x9 -> x0, matrix products: 27.1 us -> none  [the longest x1 5.68 us: body(): jnp.einsum('ste,de->std', grad_branch, full_weights[0], preferred_element...]
    pallas_call x1, Pallas kernels: 32 us -> 54.4 us  [attend_back(): pl.pallas_call(functools.partial(attend_back_kernel, heads, size, fold, n...]
    pallas_call x1, Pallas kernels: 99.1 us -> 120 us  [gather_tokens(): pl.pallas_call(functools.partial(gather_kernel, n, nb, chunks), out_shape...]
    pallas_call x1, Pallas kernels: 20.2 us -> 33.4 us  [attend(): pl.pallas_call(functools.partial(attend_kernel, heads, size, fold), grid=...]
    reshape x4 -> x0, local copies, waits for them, and re-layouts: 11.7 us -> none  [the longest x2 6.7 us: body(): grad_attended.reshape(2, fold, rows // fold, group_count, group_width)]
  transfers between devices with their start and end apart: 2 -> 0, of which waited for: 0 -> 0; matrix products, arithmetic and copies ran while one was open for 11% -> 0% of each run, Pallas kernels for 62% -> 0%
where the time goes in v2:
time: 488 us; the launch traced here: 482 us
  Pallas kernels  417 us (85%)
  local copies, waits for them, and re-layouts  25 us (5%)
  other arithmetic  18.4 us (4%)
  matrix products  17.4 us (4%)
    pallas_call x1, Pallas kernels, gather_tokens(): pl.pallas_call(functools.partial(gather_kernel, n, nb, chunks), out_shape...  120 us
    pallas_call x1, Pallas kernels, reduce_grads(): pl.pallas_call(functools.partial(reduce_kernel, n, nb, chunks), out_shape...  110 us
    pallas_call x1, Pallas kernels, attend_back(): pl.pallas_call(functools.partial(attend_back_kernel, heads, size, fold, n...  54.4 us
    pallas_call x1, Pallas kernels, layer(): pl.pallas_call(functools.partial(layer_kernel, n, nb, fold), out_shape=(j...  42.5 us
    pallas_call x1, Pallas kernels, attend(): pl.pallas_call(functools.partial(attend_kernel, heads, size, fold), grid=...  33.4 us
    pallas_call x1, Pallas kernels, swap_blocks(): pl.pallas_call(functools.partial(swap_kernel, n), out_shape=jax.ShapeDtyp...  22.6 us
    pallas_call x1, Pallas kernels, total_all(): pl.pallas_call(functools.partial(total_kernel, n, nb), out_shape=jax.Shap...  20.8 us
    pallas_call x1, Pallas kernels, project(): pl.pallas_call(functools.partial(project_kernel, heads, size), grid=(n,),...  13.1 us

profile of v2, /device:TPU:0, one launch (start us, length us, event | category | flops | bytes accessed | tf_op | source)
XLA Modules:
  0.0 482.3 jit_solution(12532767157198147758)
XLA Ops:
  0.7 1.2 dynamic_slice.6.len_ref
  1.9 1.3 convert_element_type.21
  6.1 120.3 %gather_tokens.1 = (bf16[8,256,1280]{2,1,0:T(8,128)(2,1)}, bf16[4,8,40,1024]{3,2,1,0:T(8,128)(2,1)}, bf16[4,8,3,40,1280]{4,3,2,1,0:T(8,128)(2,1)}) custom-call(bf16[2,256,1280]{2,1,0:T(8,128)(2,1)} %tok.3, bf16[4,40,1024]{2,1,0:T(8,128)(2,1)} %maximum_maximum_fusion.slab, bf16[3,40,1280]{2,1,0:T(8,128)(2,1)} %get-tuple-element.62.own_w), custom_call_target="tpu_custom_call" | custom-call | tf_op jit(solution)/shard_map/gather_tokens/pallas_call | solution.py:325
  126.4 1.1 slice_convert_fusion
  128.4 1.7 copy-done.1
  130.2 13.1 %project.1 = (bf16[8,256,1280]{2,1,0:T(8,128)(2,1)}, bf16[12,2048,128]{2,1,0:T(8,128)(2,1)}, f32[4,2048,128]{2,1,0:T(8,128)}) custom-call(bf16[8,256,1280]{2,1,0:T(8,128)(2,1)} %get-tuple-element.32.x_ref, bf16[1280,1024]{1,0:T(8,128)(2,1)S(1)} %bitcast.28, f32[1,1280]{1,0:T(1,128)S(1)} %get-tuple-element.68.gain_ref, f32[1,128]{1,0:T(1,128)S(1)} %pad_bitcast_fusion.1.coef_ref), custom_call_target="tpu_custom_call" | custom-call | tf_op jit(solution)/shard_map/project/pallas_call | solution.py:411
  143.3 33.4 %attend.1 = (bf16[8,128,640]{2,1,0:T(8,128)(2,1)S(1)}, f32[4,2048,128]{2,1,0:T(8,128)S(1)}, f32[4,8,2048]{2,1,0:T(8,128)S(1)}) custom-call(s32[1]{0:T(128)} %dynamic_slice.6.len_ref, bf16[12,2048,128]{2,1,0:T(8,128)(2,1)} %get-tuple-element.34.q_ref.k_ref.v_ref, bf16[12,2048,128]{2,1,0:T(8,128)(2,1)} %get-tuple-element.34.q_ref.k_ref.v_ref, ...), custom_call_target="tpu_custom_call" | custom-call | tf_op jit(solution)/shard_map/attend/pallas_call | solution.py:500
  176.7 2.0 copy-done
  180.4 22.6 %swap_blocks.1.o_in = bf16[8,128,640]{2,1,0:T(8,128)(2,1)} custom-call(bf16[8,128,640]{2,1,0:T(8,128)(2,1)} %copy-done.3), custom_call_target="tpu_custom_call" | custom-call | tf_op jit(solution)/shard_map/swap_blocks/pallas_call | solution.py:375
  203.0 8.5 %copy.41 = bf16[3,4,8,40,1280]{4,3,2,1,0:T(8,128)(2,1)} copy(bf16[3,4,8,40,1280]{4,3,0,2,1:T(8,128)(2,1)} %bitcast.31) | data formatting | bytes 19660800 | tf_op jit(solution)/shard_map/transpose | solution.py:1215
  211.5 42.5 %layer.1 = (bf16[2,256,1280]{2,1,0:T(8,128)(2,1)}, f32[2,256,1280]{2,1,0:T(8,128)}, bf16[8,128,640]{2,1,0:T(8,128)(2,1)}, f32[4,8,1280]{2,1,0:T(8,128)}, bf16[4,3,160,1280]{3,2,1,0:T(8,128)(2,1)}) custom-call(bf16[2,256,1280]{2,1,0:T(8,128)(2,1)} %tok.3, bf16[2,256,1280]{2,1,0:T(8,128)(2,1)} %cot.1, bf16[8,128,640]{2,1,0:T(8,128)(2,1)} %swap_blocks.1.o_in, ...), custom_call_target="tpu_custom_call" | custom-call | tf_op jit(solution)/shard_map/layer/pallas_call | solution.py:790
  254.1 54.4 %attend_back.1 = (bf16[8,256,1024]{2,1,0:T(8,128)(2,1)}, f32[8,128]{1,0:T(8,128)}) custom-call(s32[1]{0:T(128)} %dynamic_slice.6.len_ref, f32[1,128]{1,0:T(1,128)} %copy-done.5, bf16[12,2048,128]{2,1,0:T(8,128)(2,1)} %get-tuple-element.34.q_ref.k_ref.v_ref, bf16[12,2048,128]{2,1,0:T(8,128)(2,1)} %get-tuple-element.34.q_ref.k_ref.v_ref, ...), custom_call_target="tpu_custom_call" | custom-call | tf_op jit(solution)/shard_map/attend_back/pallas_call | solution.py:611
  308.5 10.0 %bitcast_convert_fusion = bf16[1280,1024]{1,0:T(8,128)(2,1)} fusion(bf16[8,256,1280]{2,1,0:T(8,128)(2,1)} %get-tuple-element.44, bf16[8,256,1024]{2,1,0:T(8,128)(2,1)} %get-tuple-element.43), kind=kOutput, calls=%fused_computation.1 | convolution fusion | flops 5370019840 | bytes 12058624 | tf_op jit(solution)/shard_map/nrd,nrc->dc/dot_general | solution.py:1238
  318.5 7.4 %convolution_convert_fusion.gh = bf16[8,256,1280]{2,1,0:T(8,128)(2,1)} fusion(bf16[8,256,1024]{2,1,0:T(8,128)(2,1)S(1)} %copy-done.20, bf16[1280,1024,1]{1,0,2:T(8,128)(2,1)S(1)} %bitcast.29), kind=kOutput, calls=%fused_computation | convolution fusion | flops 5371330560 | bytes 12058624 | tf_op jit(solution)/shard_map/nrc,dc->nrd/dot_general | solution.py:1239
  325.9 109.8 %reduce_grads.1 = (bf16[2,256,1280]{2,1,0:T(8,128)(2,1)}, f32[4,40,1024]{2,1,0:T(8,128)}, f32[3,40,1280]{2,1,0:T(8,128)}) custom-call(bf16[8,256,1280]{2,1,0:T(8,128)(2,1)} %convolution_convert_fusion.gh, bf16[4,8,40,1024]{3,2,1,0:T(8,128)(2,1)} %bitcast.33, bf16[4,3,160,1280]{3,2,1,0:T(8,128)(2,1)} %get-tuple-element.45.w_half), custom_call_target="tpu_custom_call" | custom-call | tf_op jit(solution)/shard_map/reduce_grads/pallas_call | solution.py:1073
  435.7 1.5 reshape.77
  442.9 20.8 %total_all.1 = f32[24,128]{1,0:T(8,128)} custom-call(f32[24,128]{1,0:T(8,128)} %pad_bitcast_fusion.value), custom_call_target="tpu_custom_call" | custom-call | tf_op jit(solution)/shard_map/total_all/pallas_call | solution.py:1157
  463.7 1.3 fusion.17
  465.0 1.3 slice.60
  467.5 1.3 multiply_reduce_fusion.2
  469.6 1.2 multiply_subtract_fusion.2
  471.5 4.6 multiply_subtract_fusion
  476.1 1.3 fusion.12
  477.4 2.2 fusion.4
  (73 shorter events, 12.7 us)
Async XLA Ops:
  4.0 1.0 copy-start.14
  126.4 2.0 copy-start.17
  128.4 1.7 copy-start.1
  130.2 13.1 %copy-start.5 = (f32[1,128]{1,0:T(1,128)}, f32[1,128]{1,0:T(1,128)S(1)}, u32[]{:S(2)}) copy-start(f32[1,128]{1,0:T(1,128)S(1)} %pad_bitcast_fusion.1.coef_ref) | copy-start | bytes 1540
  176.7 2.0 copy-start
  178.7 1.1 copy-start.3
  179.7 0.7 copy-start.4
  308.5 10.0 %copy-start.2 = (bf16[4,8,40,1024]{3,2,1,0:T(8,128)(2,1)S(1)}, bf16[4,8,40,1024]{3,2,1,0:T(8,128)(2,1)}, u32[]{:S(2)}) copy-start(bf16[4,8,40,1024]{3,2,1,0:T(8,128)(2,1)} %get-tuple-element.33) | copy-start | bytes 7864324
  308.5 10.0 %copy-start.20 = (bf16[8,256,1024]{2,1,0:T(8,128)(2,1)S(1)}, bf16[8,256,1024]{2,1,0:T(8,128)(2,1)}, u32[]{:S(2)}) copy-start(bf16[8,256,1024]{2,1,0:T(8,128)(2,1)} %get-tuple-element.43) | copy-start | bytes 12582916
  437.7 1.1 copy-start.11
  438.2 1.5 copy-start.6
  438.8 1.4 copy-start.7
  440.2 1.0 copy-start.13
  440.2 1.1 copy-start.12
  440.2 29.3 %copy-start.18 = (f32[80]{0:T(128)S(1)}, f32[80]{0:T(128)}, u32[]{:S(2)}) copy-start(f32[80]{0:T(128)} %param.21) | copy-start | bytes 964
  440.2 29.3 %copy-start.19 = (f32[80]{0:T(128)S(1)}, f32[80]{0:T(128)}, u32[]{:S(2)}) copy-start(f32[80]{0:T(128)} %param.22) | copy-start | bytes 964
  440.2 30.6 %copy-start.15 = (f32[2,40]{1,0:T(2,128)S(1)}, f32[2,40]{1,0:T(2,128)}, u32[]{:S(2)}) copy-start(f32[2,40]{1,0:T(2,128)} %param.19) | copy-start | bytes 964
  440.3 30.6 %copy-start.16 = (f32[2,40]{1,0:T(2,128)S(1)}, f32[2,40]{1,0:T(2,128)}, u32[]{:S(2)}) copy-start(f32[2,40]{1,0:T(2,128)} %param.20) | copy-start | bytes 964
  471.5 5.9 %copy-start.8 = (bf16[2,256,1280]{2,1,0:T(8,128)(2,1)S(1)}, bf16[2,256,1280]{2,1,0:T(8,128)(2,1)}, u32[]{:S(2)}) copy-start(bf16[2,256,1280]{2,1,0:T(8,128)(2,1)} %get-tuple-element.46) | copy-start | bytes 3932164
  471.5 5.9 %copy-start.9 = (f32[2,256,1280]{2,1,0:T(8,128)S(1)}, f32[2,256,1280]{2,1,0:T(8,128)}, u32[]{:S(2)}) copy-start(f32[2,256,1280]{2,1,0:T(8,128)} %get-tuple-element.38) | copy-start | bytes 7864324
  477.4 2.2 copy-start.10

commit v3 on v2

--- a/solution.py
+++ b/solution.py
@@ -164,9 +164,8 @@
 
 
 def gather_kernel(
-    n, nb, chunks, tok, slab, own_w, xg, wout, w_all, far_sem, own_sem, pass_sem, sib_sem, same_recv,
-    sib_recv, z_send, z_recv, b_send, b_recv, wz_send, wz_recv, wb_send, wb_recv, ws_send, ws_recv,
-    local_sem,
+    n, nb, chunks, tok, slab, xg, wout, far_sem, own_sem, pass_sem, sib_sem, same_recv, sib_recv,
+    z_send, z_recv, b_send, b_recv, local_sem,
 ):
     chips, half_chips = n // 2, n // 4
     me, core, chip, half, base, gate_mine, gate_other = place(n)
@@ -186,12 +185,6 @@
         )
         copy.start()
         z_copies.append(copy)
-    w_copies = []
-    for k in range(1, chips):
-        target = 2 * lax.rem(chip + k, chips) + core
-        copy = push(own_w, w_all.at[batch, me], wz_send.at[k], wz_recv.at[k], seq=target)
-        copy.start()
-        w_copies.append(copy)
 
     def part(ref, lead, c):
         return ref.at[lead, pl.ds(c * rows, rows)]
@@ -221,25 +214,12 @@
         slab.at[lax.rem(me, group_count)], wout.at[batch, me], local_sem.at[1]
     )
     slab_copy.start()
-    w_copy = pltpu.make_async_copy(own_w, w_all.at[batch, me], local_sem.at[2])
-    w_copy.start()
     slab_copy.wait()
-    w_copy.wait()
 
     slices = Spread(nb, wout, b_send, b_recv)
-    whole = Spread(nb, w_all, wb_send, wb_recv)
 
     def line_slot(k):
         return lax.rem(me + n - k, n)
-
-    def chip_slot(k):
-        return 2 * lax.rem(chip + chips - k, chips) + core
-
-    def to_sibling(owner, lane, slot, j):
-        block = w_all.at[owner, slot]
-        copy = push(block, block, ws_send.at[j, lane], ws_recv.at[owner, slot], seq=sibling)
-        copy.start()
-        sends.append(copy)
 
     def pass_tokens(c):
         for k in range(1, half_chips):
@@ -267,45 +247,23 @@
             sends.append(copy)
 
     slices.begin(me, 0)
-    whole.begin(me, 0)
-    to_sibling(batch, 0, me, 0)
     for k in range(1, n):
         z_copies[k - 1].wait_recv()
         slices.begin(line_slot(k), k)
     pass_tokens(0)
-    for k in range(1, chips):
-        w_copies[k - 1].wait_recv()
-        whole.begin(chip_slot(k), k)
-        to_sibling(batch, k, chip_slot(k), 0)
-    pass_tokens(1)
     for k in range(n):
         slices.relay(line_slot(k), k)
-    pass_tokens(2)
-    for k in range(chips):
-        for j, owner in enumerate(whole.relay(chip_slot(k), k)):
-            to_sibling(owner, k, chip_slot(k), 1 + j)
-    pass_tokens(3)
+    for c in range(1, chunks):
+        pass_tokens(c)
     for k in range(n):
         slices.finish(line_slot(k), k)
-    for k in range(chips):
-        owners = whole.finish(chip_slot(k), k)
-        for j, owner in enumerate(owners):
-            to_sibling(owner, k, chip_slot(k), nb - len(owners) + j)
-
     for c in range(chunks):
         for q in range(chips):
             slot = 2 * q + 1 - core
             tok_copy(part(xg, slot, c), slot, c, sib_sem.at[0, c], sib_recv, sibling).wait_recv()
-    for owner in range(nb):
-        for q in range(chips):
-            block = w_all.at[owner, 2 * q + 1 - core]
-            push(
-                block, block, ws_send.at[0, 0], ws_recv.at[owner, 2 * q + 1 - core], seq=sibling
-            ).wait_recv()
     own_copy.wait()
     slices.drain()
-    whole.drain()
-    for copy in sends + z_copies + w_copies:
+    for copy in sends + z_copies:
         copy.wait_send()
 
     @pl.when(chip == gate_mine)
@@ -318,7 +276,7 @@
                     ).wait_send()
 
 
-def gather_tokens(n, nb, tokens, slab, own_w):
+def gather_tokens(n, nb, tokens, slab):
     chunks = 4
     chips, half_chips = n // 2, n // 4
     dma = pltpu.SemaphoreType.DMA
@@ -327,10 +285,9 @@
         out_shape=(
             jax.ShapeDtypeStruct((n,) + tokens.shape[1:], tokens.dtype),
             jax.ShapeDtypeStruct((nb, n) + slab.shape[1:], slab.dtype),
-            jax.ShapeDtypeStruct((nb, n) + own_w.shape, own_w.dtype),
         ),
-        in_specs=[pl.BlockSpec(memory_space=pl.ANY)] * 3,
-        out_specs=[pl.BlockSpec(memory_space=pl.ANY)] * 3,
+        in_specs=[pl.BlockSpec(memory_space=pl.ANY)] * 2,
+        out_specs=[pl.BlockSpec(memory_space=pl.ANY)] * 2,
         scratch_shapes=[
             dma((chunks,)),
             dma((half_chips, chunks)),
@@ -342,189 +299,245 @@
             dma((n,)),
             dma((nb, n)),
             dma((nb, n)),
+            dma((2,)),
+        ],
+        compiler_params=pltpu.CompilerParams(collective_id=1, has_side_effects=True),
+        name="gather_tokens",
+    )(tokens, slab)
+
+
+def widen(values):
+    rows, width = values.shape
+    return jnp.concatenate([values, jnp.zeros((rows, LANES - width), values.dtype)], axis=1)
+
+
+def attend_kernel(
+    n, nb, heads, size, fold, len_ref, x_in, w_ref, gain_ref, coef_ref, own_w, h_out, qkv_out, q_out,
+    keep_out, lse_out, o_out, w_all, x_s, qkv_s, q_s, keep_s, o_s, s_s, m_s, acc_s, sum_s, bias_s,
+    x_sem, h_sem, qkv_sem, q_sem, keep_sem, local_sem, o_send, o_recv, wz_send, wz_recv, wb_send,
+    wb_recv, ws_send, ws_recv,
+):
+    chips = n // 2
+    me, core, chip, *_ = place(n)
+    batch = lax.axis_index("batch")
+    sibling = 2 * chip + 1 - core
+    block = x_in.shape[1]
+    group = range(heads)
+    greet(n, nb)
+
+    sends = []
+    w_copies = []
+    for k in range(1, chips):
+        target = 2 * lax.rem(chip + k, chips) + core
+        copy = push(own_w, w_all.at[batch, me], wz_send.at[k], wz_recv.at[k], seq=target)
+        copy.start()
+        w_copies.append(copy)
+    w_copy = pltpu.make_async_copy(own_w, w_all.at[batch, me], local_sem.at[0])
+    w_copy.start()
+
+    def x_load(i):
+        return pltpu.make_async_copy(x_in.at[i], x_s.at[i], x_sem.at[i])
+
+    for i in range(n):
+        x_load(i).start()
+    length = len_ref[0]
+
+    @pl.loop(0, n)
+    def _(j):
+        col = j * block + lax.broadcasted_iota(jnp.int32, (8, block), 1)
+        bias_s[j] = jnp.where(col < length, 0.0, MASKED)
+
+    whole = Spread(nb, w_all, wb_send, wb_recv)
+
+    def chip_slot(k):
+        return 2 * lax.rem(chip + chips - k, chips) + core
+
+    def to_sibling(owner, lane, slot, j):
+        piece = w_all.at[owner, slot]
+        copy = push(piece, piece, ws_send.at[j, lane], ws_recv.at[owner, slot], seq=sibling)
+        copy.start()
+        sends.append(copy)
+
+    w_copy.wait()
+    whole.begin(me, 0)
+    to_sibling(batch, 0, me, 0)
+
+    def kept(i):
+        return [
+            pltpu.make_async_copy(x_s.at[i], h_out.at[i], h_sem.at[i]),
+            pltpu.make_async_copy(qkv_s.at[i], qkv_out.at[i], qkv_sem.at[i]),
+            pltpu.make_async_copy(q_s.at[i], q_out.at[i], q_sem.at[i]),
+            pltpu.make_async_copy(keep_s.at[i], keep_out.at[i], keep_sem.at[i]),
+        ]
+
+    def o_push(i):
+        return push(o_s.at[i], o_out.at[me], o_send.at[i], o_recv.at[me], seq=i)
+
+    own_o = pltpu.make_async_copy(o_s.at[me], o_out.at[me], local_sem.at[1])
+
+    def project(i):
+        x = x_s[i].astype(F32)
+        h = (x * rms_factor(x) * gain_ref[...]).astype(LOW)
+        x_s[i] = h
+        out = dot(h, w_ref[...])
+        for a in group:
+            q = widen(out[:, a * size : (a + 1) * size])
+            q_s[i, a] = q
+            qkv_s[i, a] = (q * coef_ref[...]).astype(LOW)
+        for a in range(heads, 3 * heads):
+            qkv_s[i, a] = widen(out[:, a * size : (a + 1) * size].astype(LOW))
+
+    def score(i, j, diagonal):
+        if diagonal:
+            row = lax.broadcasted_iota(jnp.int32, (block, block), 0)
+            col = lax.broadcasted_iota(jnp.int32, (block, block), 1)
+            visible = col <= row
+        for a in group:
+            s = dot(qkv_s[i, a], qkv_s[j, heads + a], 1, 1) + bias_s[j, :1]
+            if diagonal:
+                s = jnp.where(visible, s, MASKED)
+            s_s[a, j] = s
+            best = m_s[a]
+            for part in range(block // LANES):
+                best = jnp.maximum(best, s[:, part * LANES : (part + 1) * LANES])
+            m_s[a] = best
+
+    def mix(j):
+        for a in group:
+            best = m_s[a]
+            count = sum_s[a]
+            pieces = []
+            for part in range(block // LANES):
+                e = jnp.exp(s_s[a, j, :, part * LANES : (part + 1) * LANES] - best)
+                count = count + e
+                pieces.append(e.astype(LOW))
+            sum_s[a] = count
+            acc_s[a] += dot(jnp.concatenate(pieces, axis=1), qkv_s[j, 2 * heads + a])
+
+    def query_block(i):
+        x_load(i).wait()
+        project(i)
+        m_s[...] = jnp.full_like(m_s, MASKED)
+        sum_s[...] = jnp.zeros_like(sum_s)
+        acc_s[...] = jnp.zeros_like(acc_s)
+        pl.loop(0, i)(lambda j: score(i, j, False))
+        score(i, i, True)
+        for a in group:
+            m_s[a] = jnp.broadcast_to(jnp.max(m_s[a], axis=1, keepdims=True), (block, LANES))
+        pl.loop(0, i + 1)(mix)
+        outs = []
+        for a in group:
+            count = jnp.sum(sum_s[a], axis=1, keepdims=True)
+            out = acc_s[a] / count
+            keep_s[i, a] = out
+            outs.append(out[:, :size])
+            lse_out[i, a] = (m_s[a] + jnp.log(count)).T[:8]
+        low = jnp.concatenate(outs, axis=1).astype(LOW)
+        piece = block // fold
+        o_s[i] = jnp.concatenate([low[f * piece : (f + 1) * piece] for f in range(fold)], axis=1)
+        for copy in kept(i):
+            copy.start()
+
+        @pl.when(i != me)
+        def _():
+            o_push(i).start()
+
+        @pl.when(i == me)
+        def _():
+            own_o.start()
+
+    first, second = n // 2 + 1, n - 1
+    pl.loop(0, first)(query_block)
+    for k in range(1, chips):
+        w_copies[k - 1].wait_recv()
+        whole.begin(chip_slot(k), k)
+        to_sibling(batch, k, chip_slot(k), 0)
+    if second > first:
+        pl.loop(first, second)(query_block)
+    for k in range(chips):
+        for j, owner in enumerate(whole.relay(chip_slot(k), k)):
+            to_sibling(owner, k, chip_slot(k), 1 + j)
+    pl.loop(second, n)(query_block)
+    for k in range(chips):
+        owners = whole.finish(chip_slot(k), k)
+        for j, owner in enumerate(owners):
+            to_sibling(owner, k, chip_slot(k), nb - len(owners) + j)
+
+    for k in range(1, n):
+        source = lax.rem(me + k, n)
+        push(
+            o_s.at[source], o_out.at[source], o_send.at[source], o_recv.at[source], seq=source
+        ).wait()
+    own_o.wait()
+    for owner in range(nb):
+        for q in range(chips):
+            piece = w_all.at[owner, 2 * q + 1 - core]
+            push(
+                piece, piece, ws_send.at[0, 0], ws_recv.at[owner, 2 * q + 1 - core], seq=sibling
+            ).wait_recv()
+    whole.drain()
+    for copy in sends + w_copies:
+        copy.wait_send()
+
+    @pl.loop(0, n)
+    def _(i):
+        for copy in kept(i):
+            copy.wait()
+
+
+def attend(n, nb, heads, size, fold, length, xg, wqkv, gain, coef, own_w):
+    _, rows, width = xg.shape
+    chips = n // 2
+    folded = (n, rows // fold, heads * size * fold)
+    many, one = (n, 3 * heads, rows, LANES), (n, heads, rows, LANES)
+    dma = pltpu.SemaphoreType.DMA
+    vmem = pl.BlockSpec(memory_space=pltpu.VMEM)
+    anywhere = pl.BlockSpec(memory_space=pl.ANY)
+    state = pltpu.VMEM((heads, rows, LANES), F32)
+    return pl.pallas_call(
+        functools.partial(attend_kernel, n, nb, heads, size, fold),
+        out_shape=(
+            jax.ShapeDtypeStruct(xg.shape, LOW),
+            jax.ShapeDtypeStruct(many, LOW),
+            jax.ShapeDtypeStruct(one, F32),
+            jax.ShapeDtypeStruct(one, F32),
+            jax.ShapeDtypeStruct((n, heads, 8, rows), F32),
+            jax.ShapeDtypeStruct(folded, LOW),
+            jax.ShapeDtypeStruct((nb, n) + own_w.shape, LOW),
+        ),
+        in_specs=[pl.BlockSpec(memory_space=pltpu.SMEM), anywhere, vmem, vmem, vmem, anywhere],
+        out_specs=[anywhere, anywhere, anywhere, anywhere, vmem, anywhere, anywhere],
+        scratch_shapes=[
+            pltpu.VMEM(xg.shape, LOW),
+            pltpu.VMEM(many, LOW),
+            pltpu.VMEM(one, F32),
+            pltpu.VMEM(one, F32),
+            pltpu.VMEM(folded, LOW),
+            pltpu.VMEM((heads, n, rows, rows), F32),
+            state,
+            state,
+            state,
+            pltpu.VMEM((n, 8, rows), F32),
+            dma((n,)),
+            dma((n,)),
+            dma((n,)),
+            dma((n,)),
+            dma((n,)),
+            dma((2,)),
+            dma((n,)),
+            dma((n,)),
             dma((chips,)),
             dma((chips,)),
             dma((nb, chips)),
             dma((nb, chips)),
             dma((nb, chips)),
             dma((nb, n)),
-            dma((3,)),
         ],
-        compiler_params=pltpu.CompilerParams(collective_id=1, has_side_effects=True),
-        name="gather_tokens",
-    )(tokens, slab, own_w)
-
-
-def swap_kernel(n, source, target, send_sem, recv_sem, local_sem):
-    me = lax.axis_index("seq")
-    greet(n, 1)
-    copies = []
-    for k in range(1, n):
-        other = lax.rem(me + k, n)
-        copy = push(source.at[other], target.at[me], send_sem.at[k], recv_sem.at[k], seq=other)
-        copy.start()
-        copies.append(copy)
-    own = pltpu.make_async_copy(source.at[me], target.at[me], local_sem)
-    own.start()
-    own.wait()
-    for copy in copies:
-        copy.wait()
-
-
-def swap_blocks(n, blocks, collective_id):
-    return pl.pallas_call(
-        functools.partial(swap_kernel, n),
-        out_shape=jax.ShapeDtypeStruct(blocks.shape, blocks.dtype),
-        in_specs=[pl.BlockSpec(memory_space=pl.ANY)],
-        out_specs=pl.BlockSpec(memory_space=pl.ANY),
-        scratch_shapes=[
-            pltpu.SemaphoreType.DMA((n,)),
-            pltpu.SemaphoreType.DMA((n,)),
-            pltpu.SemaphoreType.DMA,
-        ],
-        compiler_params=pltpu.CompilerParams(collective_id=collective_id, has_side_effects=True),
-        name="swap_blocks",
-    )(blocks)
-
-
-def widen(values):
-    rows, width = values.shape
-    return jnp.concatenate([values, jnp.zeros((rows, LANES - width), values.dtype)], axis=1)
-
-
-def project_kernel(heads, size, x_ref, w_ref, gain_ref, coef_ref, h_ref, qkv_ref, q_ref):
-    x = x_ref[0].astype(F32)
-    normed = x * rms_factor(x)
-    h = (normed * gain_ref[...]).astype(LOW)
-    h_ref[0] = h
-    out = dot(h, w_ref[...])
-    for a in range(heads):
-        q = widen(out[:, a * size : (a + 1) * size])
-        q_ref[a] = q
-        qkv_ref[a] = (q * coef_ref[...]).astype(LOW)
-    for a in range(heads, 3 * heads):
-        qkv_ref[a] = widen(out[:, a * size : (a + 1) * size].astype(LOW))
-
-
-def project(heads, size, xg, weights, gain, coef):
-    n, rows, width = xg.shape
-    return pl.pallas_call(
-        functools.partial(project_kernel, heads, size),
-        grid=(n,),
-        out_shape=(
-            jax.ShapeDtypeStruct(xg.shape, LOW),
-            jax.ShapeDtypeStruct((3 * heads, n * rows, LANES), LOW),
-            jax.ShapeDtypeStruct((heads, n * rows, LANES), F32),
+        compiler_params=pltpu.CompilerParams(
+            collective_id=2, has_side_effects=True, vmem_limit_bytes=62 * MIB
         ),
-        in_specs=[
-            pl.BlockSpec((1, rows, width), lambda i: (i, 0, 0)),
-            pl.BlockSpec(weights.shape, lambda i: (0, 0)),
-            pl.BlockSpec(gain.shape, lambda i: (0, 0)),
-            pl.BlockSpec(coef.shape, lambda i: (0, 0)),
-        ],
-        out_specs=[
-            pl.BlockSpec((1, rows, width), lambda i: (i, 0, 0)),
-            pl.BlockSpec((3 * heads, rows, LANES), lambda i: (0, i, 0)),
-            pl.BlockSpec((heads, rows, LANES), lambda i: (0, i, 0)),
-        ],
-        compiler_params=pltpu.CompilerParams(vmem_limit_bytes=48 * MIB),
-        name="project",
-    )(xg, weights, gain, coef)
-
-
-def attend_kernel(
-    heads, size, fold, len_ref, q_ref, k_ref, v_ref, o_ref, keep_ref, lse_ref, s_ref, m_ref, acc_ref,
-    sum_ref,
-):
-    i = pl.program_id(0)
-    block = q_ref.shape[1]
-    length = len_ref[0]
-    whole = jnp.minimum(i, length // block)
-    total = jnp.minimum(i + 1, pl.cdiv(length, block))
-    m_ref[...] = jnp.full_like(m_ref, MASKED)
-    sum_ref[...] = jnp.zeros_like(sum_ref)
-    acc_ref[...] = jnp.zeros_like(acc_ref)
-
-    def score(j, masked):
-        keys = pl.ds(pl.multiple_of(j * block, block), block)
-        if masked:
-            row = i * block + lax.broadcasted_iota(jnp.int32, (block, block), 0)
-            col = j * block + lax.broadcasted_iota(jnp.int32, (block, block), 1)
-            visible = (col <= row) & (col < length)
-        for a in range(heads):
-            s = dot(q_ref[a], k_ref[a, keys], 1, 1)
-            if masked:
-                s = jnp.where(visible, s, MASKED)
-            s_ref[a, j] = s
-            best = m_ref[a]
-            for part in range(block // LANES):
-                best = jnp.maximum(best, s[:, part * LANES : (part + 1) * LANES])
-            m_ref[a] = best
-
-    pl.loop(0, whole)(lambda j: score(j, False))
-    pl.loop(whole, total)(lambda j: score(j, True))
-    for a in range(heads):
-        m_ref[a] = jnp.broadcast_to(jnp.max(m_ref[a], axis=1, keepdims=True), (block, LANES))
-
-    @pl.loop(0, total)
-    def _(j):
-        keys = pl.ds(pl.multiple_of(j * block, block), block)
-        for a in range(heads):
-            best = m_ref[a]
-            count = sum_ref[a]
-            pieces = []
-            for part in range(block // LANES):
-                e = jnp.exp(s_ref[a, j, :, part * LANES : (part + 1) * LANES] - best)
-                count = count + e
-                pieces.append(e.astype(LOW))
-            sum_ref[a] = count
-            acc_ref[a] += dot(jnp.concatenate(pieces, axis=1), v_ref[a, keys])
-
-    outs = []
-    for a in range(heads):
-        count = jnp.sum(sum_ref[a], axis=1, keepdims=True)
-        out = acc_ref[a] / count
-        keep_ref[a] = out
-        outs.append(out[:, :size])
-        lse = m_ref[a] + jnp.log(count)
-        lse_ref[a] = lse.T[:8]
-    low = jnp.concatenate(outs, axis=1).astype(LOW)
-    piece = block // fold
-    o_ref[0] = jnp.concatenate([low[f * piece : (f + 1) * piece] for f in range(fold)], axis=1)
-
-
-def attend(heads, size, fold, length, qkv, n):
-    full = qkv.shape[1]
-    block = full // n
-    width = heads * size * fold
-    return pl.pallas_call(
-        functools.partial(attend_kernel, heads, size, fold),
-        grid=(n,),
-        out_shape=(
-            jax.ShapeDtypeStruct((n, block // fold, width), LOW),
-            jax.ShapeDtypeStruct((heads, full, LANES), F32),
-            jax.ShapeDtypeStruct((heads, 8, full), F32),
-        ),
-        in_specs=[
-            pl.BlockSpec(memory_space=pltpu.SMEM),
-            pl.BlockSpec((heads, block, LANES), lambda i: (0, i, 0)),
-            pl.BlockSpec((heads, full, LANES), lambda i: (1, 0, 0)),
-            pl.BlockSpec((heads, full, LANES), lambda i: (2, 0, 0)),
-        ],
-        out_specs=[
-            pl.BlockSpec((1, block // fold, width), lambda i: (i, 0, 0)),
-            pl.BlockSpec((heads, block, LANES), lambda i: (0, i, 0)),
-            pl.BlockSpec((heads, 8, block), lambda i: (0, 0, i)),
-        ],
-        scratch_shapes=[
-            pltpu.VMEM((heads, n, block, block), F32),
-            pltpu.VMEM((heads, block, LANES), F32),
-            pltpu.VMEM((heads, block, LANES), F32),
-            pltpu.VMEM((heads, block, LANES), F32),
-        ],
-        compiler_params=pltpu.CompilerParams(vmem_limit_bytes=48 * MIB),
         name="attend",
-    )(length, qkv, qkv, qkv)
+    )(length, xg, wqkv, gain, coef, own_w)
 
 
 def attend_back_kernel(
@@ -532,7 +545,7 @@
     out_ref, scale_ref, kt_ref, gq_ref, gqt_ref, gk_ref, gv_ref, g_ref, delta_ref,
 ):
     i = pl.program_id(0)
-    block = q_ref.shape[1]
+    block = q_ref.shape[2]
     length = len_ref[0]
     whole = jnp.minimum(i, length // block)
     total = jnp.minimum(i + 1, pl.cdiv(length, block))
@@ -547,7 +560,7 @@
         def _(j):
             keys = pl.ds(pl.multiple_of(j * block, block), block)
             for a in range(heads):
-                kt_ref[a, j] = k_ref[a, keys].T
+                kt_ref[a, j] = k_ref[j, a].T
 
     gqt_ref[...] = jnp.zeros_like(gqt_ref)
     for a in range(heads):
@@ -562,7 +575,7 @@
         )
         g_ref[a] = g
         delta_ref[a] = jnp.broadcast_to(
-            jnp.sum((g.astype(F32) * keep_ref[a]).T, axis=0, keepdims=True), (8, block)
+            jnp.sum((g.astype(F32) * keep_ref[0, a]).T, axis=0, keepdims=True), (8, block)
         )
 
     def back(j, masked):
@@ -572,13 +585,13 @@
             row = i * block + lax.broadcasted_iota(jnp.int32, (block, block), 1)
             visible = (col <= row) & (col < length)
         for a in range(heads):
-            s = dot(k_ref[a, keys], q_ref[a], 1, 1)
-            p = jnp.exp(s - lse_ref[a, :1])
+            s = dot(k_ref[j, a], q_ref[0, a], 1, 1)
+            p = jnp.exp(s - lse_ref[0, a, :1])
             if masked:
                 p = jnp.where(visible, p, 0.0)
-            dp = dot(v_ref[a, keys], g_ref[a], 1, 1)
+            dp = dot(v_ref[j, a], g_ref[a], 1, 1)
             ds = (p * (dp - delta_ref[a, :1])).astype(LOW)
-            gk_ref[a, keys] += dot(ds, q_ref[a])
+            gk_ref[a, keys] += dot(ds, q_ref[0, a])
             gv_ref[a, keys] += dot(p.astype(LOW), g_ref[a])
             gqt_ref[a] += dot(kt_ref[a, j], ds)
 
@@ -588,7 +601,7 @@
     rows = pl.ds(pl.multiple_of(i * block, block), block)
     for a in range(heads):
         grad = gqt_ref[a].T.astype(LOW).astype(F32)
-        scale_ref[...] += jnp.sum((grad * qf_ref[a]).reshape(block // 8, 8, LANES), axis=0)
+        scale_ref[...] += jnp.sum((grad * qf_ref[0, a]).reshape(block // 8, 8, LANES), axis=0)
         gq_ref[a, rows] = (grad * coef_ref[...]).astype(LOW)
 
     @pl.when(i == n - 1)
@@ -605,8 +618,8 @@
 
 
 def attend_back(heads, size, fold, length, coef, qkv, go, keep, lse, q_full, n, slab_width):
-    full = qkv.shape[1]
-    block = full // n
+    block = qkv.shape[2]
+    full = n * block
     width = heads * size * fold
     return pl.pallas_call(
         functools.partial(attend_back_kernel, heads, size, fold, n),
@@ -618,13 +631,13 @@
         in_specs=[
             pl.BlockSpec(memory_space=pltpu.SMEM),
             pl.BlockSpec(coef.shape, lambda i: (0, 0)),
-            pl.BlockSpec((heads, block, LANES), lambda i: (0, i, 0)),
-            pl.BlockSpec((heads, full, LANES), lambda i: (1, 0, 0)),
-            pl.BlockSpec((heads, full, LANES), lambda i: (2, 0, 0)),
+            pl.BlockSpec((1, heads, block, LANES), lambda i: (i, 0, 0, 0)),
+            pl.BlockSpec((n, heads, block, LANES), lambda i: (0, 1, 0, 0)),
+            pl.BlockSpec((n, heads, block, LANES), lambda i: (0, 2, 0, 0)),
             pl.BlockSpec((1, block // fold, width), lambda i: (i, 0, 0)),
-            pl.BlockSpec((heads, block, LANES), lambda i: (0, i, 0)),
-            pl.BlockSpec((heads, 8, block), lambda i: (0, 0, i)),
-            pl.BlockSpec((heads, block, LANES), lambda i: (0, i, 0)),
+            pl.BlockSpec((1, heads, block, LANES), lambda i: (i, 0, 0, 0)),
+            pl.BlockSpec((1, heads, 8, block), lambda i: (i, 0, 0, 0)),
+            pl.BlockSpec((1, heads, block, LANES), lambda i: (i, 0, 0, 0)),
         ],
         out_specs=[
             pl.BlockSpec((n, block, slab_width), lambda i: (0, 0, 0)),
@@ -1211,17 +1224,17 @@
     spare = jnp.zeros((group_count, shard, slab_width - 3 * group_width - 2), LOW)
     slab = jnp.concatenate([slab, low_gains, spare], axis=2)
 
-    xg, wout, w_all = gather_tokens(n, nb, tokens, slab, low_weights[3:])
-    w_all = w_all.transpose(2, 0, 1, 3, 4).reshape(3, width, width)
+    xg, wout = gather_tokens(n, nb, tokens, slab)
     wqkv = wout.reshape(nb * n * shard, slab_width)
     gain_rows = wqkv[:, 3 * group_width : 3 * group_width + 2].astype(F32).T
     gain_one, gain_two = gain_rows[0:1], gain_rows[1:2]
 
     coef = LOG_TWO_E / math.sqrt(size) * jax.nn.softplus(query_scale)
     coef_row = jnp.concatenate([coef, jnp.zeros((LANES - size,), F32)])[None]
-    normed_in, qkv, q_full = project(heads, size, xg, wqkv, gain_one, coef_row)
-    o_send, o_keep, lse = attend(heads, size, fold, length, qkv, n)
-    o_recv = swap_blocks(n, o_send, 2)
+    normed_in, qkv, q_full, o_keep, lse, o_recv, w_all = attend(
+        n, nb, heads, size, fold, length, xg, wqkv, gain_one, coef_row, low_weights[3:]
+    )
+    w_all = w_all.transpose(2, 0, 1, 3, 4).reshape(3, width, width)
     block_out, grad_middle, go_recv, layer_sums, w_half = layer(
         n, nb, fold, tokens, cotangent, o_recv, w_all, gain_two
     )

time: 488 us -> 437 us (0.90)
  Pallas kernels: 417 us -> 369 us
  local copies, waits for them, and re-layouts: 25 us -> 20 us
    pallas_call x1, Pallas kernels: 120 us -> 70.9 us  [gather_tokens(): pl.pallas_call(functools.partial(gather_kernel, n, nb, chunks), out_shape...]
    pallas_call x1, Pallas kernels: 42.5 us -> 36.7 us  [layer(): pl.pallas_call(functools.partial(layer_kernel, n, nb, fold), out_shape=(j...]
    unnamed x45 -> x35, local copies, waits for them, and re-layouts: 7.54 us -> 2.06 us
    pallas_call x3 -> x1, Pallas kernels: 69.1 us -> 74.1 us  [attend(): pl.pallas_call(functools.partial(attend_kernel, n, nb, heads, size, fold)...]
where the time goes in v3:
time: 437 us; the launch traced here: 429 us
  Pallas kernels  369 us (84%)
  local copies, waits for them, and re-layouts  20 us (5%)
  other arithmetic  18.4 us (4%)
  matrix products  17.4 us (4%)
  between operations  4.51 us (1%)
    pallas_call x1, Pallas kernels, reduce_grads(): pl.pallas_call(functools.partial(reduce_kernel, n, nb, chunks), out_shape...  112 us
    pallas_call x1, Pallas kernels, attend(): pl.pallas_call(functools.partial(attend_kernel, n, nb, heads, size, fold)...  74.1 us
    pallas_call x1, Pallas kernels, gather_tokens(): pl.pallas_call(functools.partial(gather_kernel, n, nb, chunks), out_shape...  70.9 us
    pallas_call x1, Pallas kernels, attend_back(): pl.pallas_call(functools.partial(attend_back_kernel, heads, size, fold, n...  54.5 us
    pallas_call x1, Pallas kernels, layer(): pl.pallas_call(functools.partial(layer_kernel, n, nb, fold), out_shape=(j...  36.7 us
    pallas_call x1, Pallas kernels, total_all(): pl.pallas_call(functools.partial(total_kernel, n, nb), out_shape=jax.Shap...  19.9 us
    dot_general x1, matrix products, body(): jnp.einsum('nrd,nrc->dc', normed_in, grad_proj, preferred_element_type=F32)  10 us

profile of v3, /device:TPU:0, one launch (start us, length us, event | category | flops | bytes accessed | tf_op | source)
XLA Modules:
  0.0 428.9 jit_solution(8802060985825583739)
XLA Ops:
  0.7 1.2 dynamic_slice.6.len_ref
  1.9 1.3 convert_element_type.21
  5.3 0.8 maximum_maximum_fusion.slab
  6.1 70.9 %gather_tokens.1 = (bf16[8,256,1280]{2,1,0:T(8,128)(2,1)}, bf16[4,8,40,1024]{3,2,1,0:T(8,128)(2,1)}) custom-call(bf16[2,256,1280]{2,1,0:T(8,128)(2,1)} %tok.3, bf16[4,40,1024]{2,1,0:T(8,128)(2,1)} %maximum_maximum_fusion.slab), custom_call_target="tpu_custom_call" | custom-call | tf_op jit(solution)/shard_map/gather_tokens/pallas_call | solution.py:283
  77.0 1.1 slice_convert_fusion
  79.5 74.1 %attend.1 = (bf16[8,256,1280]{2,1,0:T(8,128)(2,1)}, bf16[8,12,256,128]{3,2,1,0:T(8,128)(2,1)}, f32[8,4,256,128]{3,2,1,0:T(8,128)}, f32[8,4,256,128]{3,2,1,0:T(8,...) custom-call(s32[1]{0:T(128)} %dynamic_slice.6.len_ref, ...), custom_call_target="tpu_custom_call" | custom-call | tf_op jit(solution)/shard_map/attend/pallas_call | solution.py:497
  153.6 8.5 %copy.41 = bf16[3,4,8,40,1280]{4,3,2,1,0:T(8,128)(2,1)} copy(bf16[3,4,8,40,1280]{4,3,0,2,1:T(8,128)(2,1)} %bitcast.28) | data formatting | bytes 19660800 | tf_op jit(solution)/shard_map/transpose | solution.py:1237
  162.1 36.7 %layer.1 = (bf16[2,256,1280]{2,1,0:T(8,128)(2,1)}, f32[2,256,1280]{2,1,0:T(8,128)}, bf16[8,128,640]{2,1,0:T(8,128)(2,1)}, f32[4,8,1280]{2,1,0:T(8,128)}, bf16[4,3,160,1280]{3,2,1,0:T(8,128)(2,1)}) custom-call(bf16[2,256,1280]{2,1,0:T(8,128)(2,1)} %tok.3, bf16[2,256,1280]{2,1,0:T(8,128)(2,1)} %cot.1, bf16[8,128,640]{2,1,0:T(8,128)(2,1)} %get-tuple-element.34.o_in, ...), custom_call_target="tpu_custom_call" | custom-call | tf_op jit(solution)/shard_map/layer/pallas_call | solution.py:803
  198.9 54.5 %attend_back.1 = (bf16[8,256,1024]{2,1,0:T(8,128)(2,1)}, f32[8,128]{1,0:T(8,128)}) custom-call(s32[1]{0:T(128)} %dynamic_slice.6.len_ref, f32[1,128]{1,0:T(1,128)} %pad_bitcast_fusion.1.coef_ref, bf16[8,12,256,128]{3,2,1,0:T(8,128)(2,1)} %get-tuple-element.38.q_ref.k_ref.v_ref, bf16[8,12,256,128]{3,2,1,0:T(8,128)(2,1)} %get-tuple-element.38.q_ref.k_ref.v_ref, ...), custom_call_target="tpu_custom_call" | custom-call | tf_op jit(solution)/shard_map/attend_back/pallas_call | solution.py:624
  253.3 10.0 %bitcast_convert_fusion = bf16[1280,1024]{1,0:T(8,128)(2,1)} fusion(bf16[8,256,1280]{2,1,0:T(8,128)(2,1)} %get-tuple-element.44, bf16[8,256,1024]{2,1,0:T(8,128)(2,1)} %get-tuple-element.43), kind=kOutput, calls=%fused_computation.1 | convolution fusion | flops 5370019840 | bytes 12058624 | tf_op jit(solution)/shard_map/nrd,nrc->dc/dot_general | solution.py:1251
  263.4 7.4 %convolution_convert_fusion.gh = bf16[8,256,1280]{2,1,0:T(8,128)(2,1)} fusion(bf16[8,256,1024]{2,1,0:T(8,128)(2,1)S(1)} %copy-done.15, bf16[1280,1024,1]{1,0,2:T(8,128)(2,1)S(1)} %bitcast.32), kind=kOutput, calls=%fused_computation | convolution fusion | flops 5371330560 | bytes 12058624 | tf_op jit(solution)/shard_map/nrc,dc->nrd/dot_general | solution.py:1252
  270.7 112.4 %reduce_grads.1 = (bf16[2,256,1280]{2,1,0:T(8,128)(2,1)}, f32[4,40,1024]{2,1,0:T(8,128)}, f32[3,40,1280]{2,1,0:T(8,128)}) custom-call(bf16[8,256,1280]{2,1,0:T(8,128)(2,1)} %convolution_convert_fusion.gh, bf16[4,8,40,1024]{3,2,1,0:T(8,128)(2,1)} %bitcast.33, bf16[4,3,160,1280]{3,2,1,0:T(8,128)(2,1)} %get-tuple-element.45.w_half), custom_call_target="tpu_custom_call" | custom-call | tf_op jit(solution)/shard_map/reduce_grads/pallas_call | solution.py:1086
  383.2 1.5 reshape.77
  386.4 0.9 multiply_reduce_fusion
  387.8 1.0 fusion.7
  390.4 19.9 %total_all.1 = f32[24,128]{1,0:T(8,128)} custom-call(f32[24,128]{1,0:T(8,128)} %pad_bitcast_fusion.value), custom_call_target="tpu_custom_call" | custom-call | tf_op jit(solution)/shard_map/total_all/pallas_call | solution.py:1170
  410.3 1.3 fusion.17
  411.6 1.3 slice.60
  414.2 1.3 multiply_reduce_fusion.2
  416.2 1.2 multiply_subtract_fusion.2
  418.1 4.6 %multiply_subtract_fusion = (f32[6,40,1280]{2,1,0:T(8,128)}, f32[6,40,1280]{2,1,0:T(8,128)}, f32[6,40,1280]{2,1,0:T(8,128)}) fusion(f32[6,40,1280]{2,1,0:T(8,128)} %param.14, f32[6,40,1280]{2,1,0:T(8,128)S(1)} %constant_dynamic-update-slice_fusion, f32[]{:T(128)S(6)} %div.74, f32[6,40,1280]{2,1,0:T(8,128)} %param.17, f32[6,40,1280]{2,1,0:T(8,128)} %param.18), kind=kLoop, calls=%fused_computation.16 | loop fusion | flops 4915200 | bytes 8601604 | tf_op jit(solution)/shard_map/sub | solution.py:49
  422.7 1.3 fusion.12
  424.0 2.2 fusion.4
  426.2 1.1 copy.51
  (61 shorter events, 7.7 us)
Async XLA Ops:
  4.0 1.0 copy-start.9
  6.1 72.9 %copy-start.12 = (f32[80]{0:T(128)S(1)}, f32[80]{0:T(128)}, u32[]{:S(2)}) copy-start(f32[80]{0:T(128)} %param.16) | copy-start | bytes 964
  253.3 10.0 %copy-start.3 = (bf16[4,8,40,1024]{3,2,1,0:T(8,128)(2,1)S(1)}, bf16[4,8,40,1024]{3,2,1,0:T(8,128)(2,1)}, u32[]{:S(2)}) copy-start(bf16[4,8,40,1024]{3,2,1,0:T(8,128)(2,1)} %get-tuple-element.33) | copy-start | bytes 7864324
  253.3 10.0 %copy-start.15 = (bf16[8,256,1024]{2,1,0:T(8,128)(2,1)S(1)}, bf16[8,256,1024]{2,1,0:T(8,128)(2,1)}, u32[]{:S(2)}) copy-start(bf16[8,256,1024]{2,1,0:T(8,128)(2,1)} %get-tuple-element.43) | copy-start | bytes 12582916
  385.2 1.1 copy-start.6
  385.8 1.5 copy-start
  386.3 1.4 copy-start.1
  387.8 1.0 copy-start.8
  387.8 1.1 copy-start.7
  387.8 28.4 %copy-start.13 = (f32[80]{0:T(128)S(1)}, f32[80]{0:T(128)}, u32[]{:S(2)}) copy-start(f32[80]{0:T(128)} %param.21) | copy-start | bytes 964
  387.8 28.4 %copy-start.14 = (f32[80]{0:T(128)S(1)}, f32[80]{0:T(128)}, u32[]{:S(2)}) copy-start(f32[80]{0:T(128)} %param.22) | copy-start | bytes 964
  387.8 29.7 %copy-start.10 = (f32[2,40]{1,0:T(2,128)S(1)}, f32[2,40]{1,0:T(2,128)}, u32[]{:S(2)}) copy-start(f32[2,40]{1,0:T(2,128)} %param.19) | copy-start | bytes 964
  387.8 29.7 %copy-start.11 = (f32[2,40]{1,0:T(2,128)S(1)}, f32[2,40]{1,0:T(2,128)}, u32[]{:S(2)}) copy-start(f32[2,40]{1,0:T(2,128)} %param.20) | copy-start | bytes 964
  418.1 5.9 %copy-start.2 = (bf16[2,256,1280]{2,1,0:T(8,128)(2,1)S(1)}, bf16[2,256,1280]{2,1,0:T(8,128)(2,1)}, u32[]{:S(2)}) copy-start(bf16[2,256,1280]{2,1,0:T(8,128)(2,1)} %get-tuple-element.46) | copy-start | bytes 3932164
  418.1 5.9 %copy-start.4 = (f32[2,256,1280]{2,1,0:T(8,128)S(1)}, f32[2,256,1280]{2,1,0:T(8,128)}, u32[]{:S(2)}) copy-start(f32[2,256,1280]{2,1,0:T(8,128)} %get-tuple-element.37) | copy-start | bytes 7864324
  424.0 2.2 copy-start.5
